TPU v7x, 32 devices: a whole 2x2x4 slice. The times are simulated.
32 devices in a mesh: dp: 8 (over y, x, core), mp: 4 (over z).
Axes of the slice: x: 2, y: 2, z: 4, core: 2. Of those that a mesh axis runs over, the one named last changes fastest.
Arguments:
- patches: bfloat16 [32, 529, 768], P('dp'), may hold values from -6 to 6
- fill_lengths: int32 [32], P('dp'), may hold values from 33 to 529
- cotangent: bfloat16 [32, 529, 768], P('dp'), may hold values from -6 to 6
- norm1_gain: float32 [768], replicated, may hold values from 0.5 to 1.5
- norm1_shift: float32 [768], replicated, may hold values from -2 to 2
- w_qkv: bfloat16 [768, 3, 768], P(None, None, 'mp'), may hold values from -0.21875 to 0.21875
- qv_bias: float32 [2, 768], P(None, 'mp'), may hold values from -0.4 to 0.4
- w_out: bfloat16 [768, 768], P('mp'), may hold values from -1.5 to 1.5
- out_bias: float32 [768], replicated, may hold values from -2 to 2
- norm2_gain: float32 [768], replicated, may hold values from 0.5 to 1.5
- norm2_shift: float32 [768], replicated, may hold values from -2 to 2
- w_up: bfloat16 [768, 3072], P(None, 'mp'), may hold values from -0.21875 to 0.21875
- up_bias: float32 [3072], P('mp'), may hold values from -2 to 2
- w_down: bfloat16 [3072, 768], P('mp'), may hold values from -0.15625 to 0.15625
- down_bias: float32 [768], replicated, may hold values from -2 to 2
Outputs:
- layer_out: bfloat16 [32, 529, 768], P('dp')
- patches_grad: float32 [32, 529, 768], P('dp')
- norm1_gain_grad: float32 [768], P('dp')
- norm1_shift_grad: float32 [768], P('dp')
- w_qkv_grad: float32 [768, 3, 768], P('dp', None, 'mp')
- qv_bias_grad: float32 [2, 768], P(None, ('mp', 'dp'))
- w_out_grad: float32 [768, 768], P('mp', 'dp')
- out_bias_grad: float32 [768], P('dp')
- norm2_gain_grad: float32 [768], P('dp')
- norm2_shift_grad: float32 [768], P('dp')
- w_up_grad: float32 [768, 3072], P('dp', 'mp')
- up_bias_grad: float32 [3072], P(('mp', 'dp'))
- w_down_grad: float32 [3072, 768], P('mp', 'dp')
- down_bias_grad: float32 [768], P('dp')
Inputs may be any that keep to these rules, and one draw needn't show every extreme that they name: Patches of item i at positions fill_lengths[i] and beyond are not keys.
All inputs are finite; a program needn't handle non-finite values.
Results may differ from a plain program's by a relative error of at most 0.012.
Values may be sent and summed in bfloat16 or wider, within the bound.
A program may use at most 192 MiB of HBM per device.

v0:
```python
import jax
import jax.numpy as jnp
from jax import lax
from jax.sharding import PartitionSpec as P

HD = 64


epsilon = 1e-06


def normalize(values, gain, shift):
    center = values - jnp.mean(values, axis=-1, keepdims=True)
    inverse = lax.rsqrt(jnp.mean(center * center, axis=-1, keepdims=True) + epsilon)
    unit = center * inverse
    return (unit, inverse, unit * gain + shift)


def normalize_back(upstream, unit, inverse, gain):
    gain_grad = jnp.sum(upstream * unit, axis=(0, 1))
    shift_grad = jnp.sum(upstream, axis=(0, 1))
    scaled = upstream * gain
    result = inverse * (
        scaled
        - jnp.mean(scaled, axis=-1, keepdims=True)
        - unit * jnp.mean(scaled * unit, axis=-1, keepdims=True)
    )
    return (gain_grad, shift_grad, result)


def split_heads(rows):
    return rows.reshape(rows.shape[0], rows.shape[1] // HD, HD)


def masked_scores(queries, keyset, usable):
    scores = jnp.einsum("qhd,khd->hqk", queries, keyset, preferred_element_type=jnp.float32)
    return jnp.where(usable[None, None, :], scores, -1e30)


def attend(operands):
    query_rows, key_rows, value_rows, usable = operands
    scores = masked_scores(split_heads(query_rows), split_heads(key_rows), usable)
    peak = jnp.max(scores, axis=-1, keepdims=True)
    expsum = jnp.exp(scores - peak)
    total = jnp.sum(expsum, axis=-1, keepdims=True)
    weights = (expsum / total).astype(jnp.bfloat16)
    mixed = jnp.einsum(
        "hqk,khd->qhd", weights, split_heads(value_rows), preferred_element_type=jnp.float32
    )
    return (
        mixed.reshape(query_rows.shape).astype(jnp.bfloat16),
        peak[..., 0] + jnp.log(total[..., 0]),
    )


def attend_back(operands):
    query_rows, key_rows, value_rows, usable, logsum, upstream = operands
    queries = split_heads(query_rows)
    keyset = split_heads(key_rows)
    scores = masked_scores(queries, keyset, usable)
    probs = jnp.exp(scores - logsum[..., None])
    weights = probs.astype(jnp.bfloat16)
    grad_heads = split_heads(upstream)
    value_grad = jnp.einsum("hqk,qhd->khd", weights, grad_heads, preferred_element_type=jnp.float32)
    prob_grad = jnp.einsum(
        "qhd,khd->hqk", grad_heads, split_heads(value_rows), preferred_element_type=jnp.float32
    )
    center = jnp.sum(probs * prob_grad, axis=-1, keepdims=True)
    score_grad = (probs * (prob_grad - center)).astype(jnp.bfloat16)
    query_grad = jnp.einsum("hqk,khd->qhd", score_grad, keyset, preferred_element_type=jnp.float32)
    key_grad = jnp.einsum("hqk,qhd->khd", score_grad, queries, preferred_element_type=jnp.float32)
    shape = query_rows.shape
    return (
        query_grad.reshape(shape).astype(jnp.bfloat16),
        key_grad.reshape(shape).astype(jnp.bfloat16),
        value_grad.reshape(shape).astype(jnp.bfloat16),
    )


def shards(
    patches,
    fill_lengths,
    cotangent,
    norm1_gain,
    norm1_shift,
    w_qkv,
    qv_bias,
    w_out,
    out_bias,
    norm2_gain,
    norm2_shift,
    w_up,
    up_bias,
    w_down,
    down_bias,
):
    scaling = HD ** (-0.5)
    seq_len = patches.shape[1]
    inputs = patches.astype(jnp.float32)
    unit1, inverse1, normed1_full = normalize(inputs, norm1_gain, norm1_shift)
    normed1 = normed1_full.astype(jnp.bfloat16)
    projected = jnp.einsum("isd,dtc->istc", normed1, w_qkv, preferred_element_type=jnp.float32)
    queries = ((projected[:, :, 0] + qv_bias[0]) * scaling).astype(jnp.bfloat16)
    key_rows = projected[:, :, 1].astype(jnp.bfloat16)
    value_rows = (projected[:, :, 2] + qv_bias[1]).astype(jnp.bfloat16)
    usable = jnp.arange(seq_len, dtype=jnp.int32)[None, :] < fill_lengths[:, None]
    heads_out, logsum = lax.map(attend, (queries, key_rows, value_rows, usable))
    partial_attn = jnp.einsum("isc,cd->isd", heads_out, w_out, preferred_element_type=jnp.float32)
    attention = lax.psum(partial_attn, "mp")
    residual1 = inputs + attention + out_bias
    unit2, inverse2, normed2_full = normalize(residual1, norm2_gain, norm2_shift)
    normed2 = normed2_full.astype(jnp.bfloat16)
    preact = jnp.einsum("isd,df->isf", normed2, w_up, preferred_element_type=jnp.float32) + up_bias
    activated, gelu_back = jax.vjp(jax.nn.gelu, preact)
    hidden = activated.astype(jnp.bfloat16)
    partial_ff = jnp.einsum("isf,fd->isd", hidden, w_down, preferred_element_type=jnp.float32)
    feedforward = lax.psum(partial_ff, "mp")
    layer_out = (residual1 + feedforward + down_bias).astype(jnp.bfloat16)
    upstream = cotangent.astype(jnp.float32)
    down_bias_grad = jnp.sum(upstream, axis=(0, 1))
    w_down_grad = jnp.einsum("isf,isd->fd", hidden, cotangent, preferred_element_type=jnp.float32)
    hidden_grad = jnp.einsum("isd,fd->isf", cotangent, w_down, preferred_element_type=jnp.float32)
    preact_grad = gelu_back(hidden_grad)[0].astype(jnp.bfloat16)
    up_bias_grad = jnp.sum(preact_grad.astype(jnp.float32), axis=(0, 1))
    w_up_grad = jnp.einsum("isd,isf->df", normed2, preact_grad, preferred_element_type=jnp.float32)
    partial_norm2 = jnp.einsum("isf,df->isd", preact_grad, w_up, preferred_element_type=jnp.float32)
    normed2_grad = lax.psum(partial_norm2, "mp")
    norm2_gain_grad, norm2_shift_grad, through_norm2 = normalize_back(
        normed2_grad, unit2, inverse2, norm2_gain
    )
    residual1_grad = upstream + through_norm2
    out_bias_grad = jnp.sum(residual1_grad, axis=(0, 1))
    residual_low = residual1_grad.astype(jnp.bfloat16)
    w_out_grad = jnp.einsum(
        "isc,isd->cd", heads_out, residual_low, preferred_element_type=jnp.float32
    )
    heads_grad = jnp.einsum(
        "isd,cd->isc", residual_low, w_out, preferred_element_type=jnp.float32
    ).astype(jnp.bfloat16)
    query_grad, key_grad, value_grad = lax.map(
        attend_back, (queries, key_rows, value_rows, usable, logsum, heads_grad)
    )
    query_scaled = query_grad * scaling
    proj_grad = jnp.stack([query_scaled, key_grad, value_grad], axis=2)
    w_qkv_grad = jnp.einsum("isd,istc->dtc", normed1, proj_grad, preferred_element_type=jnp.float32)
    qv_bias_grad = jnp.stack(
        [
            jnp.sum(query_scaled.astype(jnp.float32), axis=(0, 1)),
            jnp.sum(value_grad.astype(jnp.float32), axis=(0, 1)),
        ]
    )
    partial_norm1 = jnp.einsum(
        "istc,dtc->isd", proj_grad, w_qkv, preferred_element_type=jnp.float32
    )
    normed1_grad = lax.psum(partial_norm1, "mp")
    norm1_gain_grad, norm1_shift_grad, through_norm1 = normalize_back(
        normed1_grad, unit1, inverse1, norm1_gain
    )
    patches_grad = residual1_grad + through_norm1
    summed = (
        lax.psum_scatter(norm1_gain_grad, "dp", scatter_dimension=0, tiled=True),
        lax.psum_scatter(norm1_shift_grad, "dp", scatter_dimension=0, tiled=True),
        lax.psum_scatter(w_qkv_grad, "dp", scatter_dimension=0, tiled=True),
        lax.psum_scatter(qv_bias_grad, "dp", scatter_dimension=1, tiled=True),
        lax.psum_scatter(w_out_grad, "dp", scatter_dimension=1, tiled=True),
        lax.psum_scatter(out_bias_grad, "dp", scatter_dimension=0, tiled=True),
        lax.psum_scatter(w_up_grad, "dp", scatter_dimension=0, tiled=True),
        lax.psum_scatter(up_bias_grad, "dp", scatter_dimension=0, tiled=True),
        lax.psum_scatter(w_down_grad, "dp", scatter_dimension=1, tiled=True),
        lax.psum_scatter(down_bias_grad, "dp", scatter_dimension=0, tiled=True),
        lax.psum_scatter(norm2_gain_grad, "dp", scatter_dimension=0, tiled=True),
        lax.psum_scatter(norm2_shift_grad, "dp", scatter_dimension=0, tiled=True),
    )
    return (
        layer_out,
        patches_grad,
        summed[0],
        summed[1],
        summed[2],
        summed[3],
        summed[4],
        summed[5],
        summed[10],
        summed[11],
        summed[6],
        summed[7],
        summed[8],
        summed[9],
    )


def solution(mesh):
    return jax.shard_map(
        shards,
        mesh=mesh,
        in_specs=(
            P("dp", None, None),
            P("dp"),
            P("dp", None, None),
            P(),
            P(),
            P(None, None, "mp"),
            P(None, "mp"),
            P("mp", None),
            P(),
            P(),
            P(),
            P(None, "mp"),
            P("mp"),
            P("mp", None),
            P(),
        ),
        out_specs=(
            P("dp", None, None),
            P("dp", None, None),
            P("dp"),
            P("dp"),
            P("dp", None, "mp"),
            P(None, ("mp", "dp")),
            P("mp", "dp"),
            P("dp"),
            P("dp"),
            P("dp"),
            P("dp", "mp"),
            P(("mp", "dp")),
            P("mp", "dp"),
            P("dp"),
        ),
        check_vma=False,
    )
```

profile of v0, /device:TPU:0, one launch (start us, length us, event | category | flops | bytes accessed | tf_op | source)
XLA Modules:
  0.0 1199.9 jit_solution(7938514547854650088)
XLA Ops:
  14.3 5.0 fusion.67
  21.7 18.7 %while.26 = (s32[]{:T(128)}, bf16[4,529,192]{1,2,0:T(8,128)(2,1)}, f32[4,3,529]{2,1,0:T(4,128)S(1)}, bf16[4,529,192]{1,2,0:T(8,128)(2,1)S(1)}, pred[4,529]{1,0:T...) while((s32[]{:T(128)}, bf16[4,529,192]{1,2,0:T(8,128)(2,1)}, ...), condition=%wide.region_5.6_spmd, body=%wide.region_2.5_spmd.sunk | while | flops 222573584 | bytes 12619750 | solution.py:107
  40.4 5.0 fusion.72
  46.0 234.7 %all-reduce.14.cloned.1.call-done = f32[4,529,768]{2,1,0:T(8,128)} async-done(((f32[4,529,768]{2,1,0:T(8,128)}), f32[4,529,768]{2,1,0:T(8,128)}) %all-reduce.14.cloned.1.call-update) | async-done | bytes 6500368 | tf_op jit(solution)/shard_map/psum | solution.py:109
  280.7 4.6 fusion.77
  291.0 7.5 convert_reduce_fusion.2
  300.3 4.7 fusion.61
  305.2 9.8 fusion.59
  315.0 221.4 %all-reduce.16.cloned.1.call-done = f32[4,529,768]{2,1,0:T(8,128)} async-done(((f32[4,529,768]{2,1,0:T(8,128)}), f32[4,529,768]{2,1,0:T(8,128)}) %all-reduce.16.cloned.1.call-update) | async-done | bytes 6500368 | tf_op jit(solution)/shard_map/psum | solution.py:127
  536.5 6.3 multiply_reduce_fusion.1
  544.1 5.1 fusion.76
  554.5 5.1 fusion.52
  562.9 37.5 %while.27 = (s32[]{:T(128)}, bf16[4,529,192]{1,2,0:T(8,128)(2,1)}, bf16[4,529,192]{1,2,0:T(8,128)(2,1)}, bf16[4,529,192]{1,2,0:T(8,128)(2,1)}, bf16[4,529,192]{1...) while((s32[]{:T(128)}, bf16[4,529,192]{1,2,0:T(8,128)(2,1)}, ...), condition=%wide.region_15.16_spmd, body=%wide.region_13.15_spmd.sunk | while | flops 547672064 | bytes 30236056 | solution.py:140
  601.8 7.6 convolution_bitcast_fusion
  609.7 9.1 fusion.45
  619.0 8.9 convolution_bitcast_fusion.2
  630.9 8.2 convolution_bitcast_fusion.1
  640.8 413.6 %all-reduce.18.cloned.1.call-done = (f32[4,529,768]{2,1,0:T(8,128)}, f32[4,529,768]{2,1,0:T(8,128)}) async-done(((f32[4,529,768]{2,1,0:T(8,128)}, f32[4,529,768]{2,1,0:T(8,128)}), (f32[4,529,768]{2,1,0:T(8,128)}, f32[4,529,768]{2,1,0:T(8,128)})) %all-reduce.18.cloned.1.call-update) | async-done | bytes 13000720 | tf_op jit(solution)/shard_map/psum | solution.py:117
  1054.4 5.9 add_convert_fusion
  1066.8 24.7 %all-reduce.8 = (f32[768]{0:T(1024)S(1)}, f32[768]{0:T(1024)S(1)}, f32[2,192]{1,0:T(2,128)S(1)}, f32[768]{0:T(1024)S(1)}, f32[768]{0:T(1024)S(1)}, /*index=5*/f3...) all-reduce(f32[768]{0:T(1024)S(1)} %get-tuple-element.141, ...), channel_id=2, replica_groups=mesh['dp'=8,'mp'=4] {'dp'}, use_global_device_ids=true, to_apply=%region_20.21.clone | all-reduce | flops 5760 | bytes 46080
  1095.6 7.0 fusion.25
  1102.6 5.3 copy.50
  1108.6 37.9 %reduce-scatter.10.cloned.1.call-done = f32[96,768]{1,0:T(8,128)} async-done(((f32[768,768]{1,0:T(8,128)}), f32[96,768]{1,0:T(8,128)}) %reduce-scatter.10.cloned.1.call-update) | async-done | bytes 294928 | tf_op jit(solution)/shard_map/reduce_scatter | solution.py:167
  1146.4 46.4 %reduce-scatter.8.cloned.1.call-done = f32[96,3,192]{2,0,1:T(8,128)} async-done(((f32[768,3,192]{2,0,1:T(8,128)}), f32[96,3,192]{2,0,1:T(8,128)}) %reduce-scatter.8.cloned.1.call-update) | async-done | bytes 221200 | tf_op jit(solution)/shard_map/reduce_scatter | solution.py:163
  (203 shorter events, 99.6 us)
Async XLA Ops:
  7.2 283.8 %copy-start = (bf16[768,768]{1,0:T(8,128)(2,1)S(1)}, bf16[768,768]{1,0:T(8,128)(2,1)}, u32[]{:S(2)}) copy-start(bf16[768,768]{1,0:T(8,128)(2,1)} %param.32) | copy-start | bytes 3538948
  7.2 273.5 %all-reduce.14.cloned.1.call-start = ((), (), s32[]{:S(2)}) async-start(), calls=%async_computation.4 | async-start | bytes 13172736 | tf_op jit(solution)/shard_map/psum | solution.py:109
  11.2 8.0 copy-start.15
  21.7 18.7 %copy-start.12 = (bf16[192,768]{1,0:T(8,128)(2,1)S(1)}, bf16[192,768]{1,0:T(8,128)(2,1)}, u32[]{:S(2)}) copy-start(bf16[192,768]{1,0:T(8,128)(2,1)} %param.26) | copy-start | bytes 884740
  40.4 240.3 %copy-start.22 = (f32[768]{0:T(1024)S(1)}, f32[768]{0:T(1024)}, u32[]{:S(2)}) copy-start(f32[768]{0:T(1024)} %param.27) | copy-start | bytes 9220
  45.4 491.0 %all-reduce.16.cloned.1.call-start = ((), (), s32[]{:S(2)}) async-start(), calls=%async_computation.5 | async-start | bytes 13172736 | tf_op jit(solution)/shard_map/psum | solution.py:127
  305.0 334.1 %reduce-scatter.14.cloned.1.call-start = ((), (), s32[]{:S(2)}) async-start(), calls=%async_computation.9 | async-start | bytes 884736
  544.1 7.9 copy-start.8
  559.6 494.8 %all-reduce.18.cloned.1.call-start = ((), (), s32[]{:S(2)}) async-start(), calls=%async_computation.10 | async-start | bytes 26345472 | tf_op jit(solution)/shard_map/psum | solution.py:117
  601.8 7.6 copy-start.14
  609.4 499.1 %reduce-scatter.12.cloned.1.call-start = ((), (), s32[]{:S(2)}) async-start(), calls=%async_computation.8 | async-start | bytes 2654208 | tf_op jit(solution)/shard_map/reduce_scatter | solution.py:169
  618.8 9.6 copy-start.28
  618.8 11.5 copy-start.9
  618.8 11.8 copy-start.7
  618.8 12.0 %copy-start.13 = (bf16[4,529,192]{1,2,0:T(8,128)(2,1)S(1)}, bf16[4,529,192]{1,2,0:T(8,128)(2,1)}, u32[]{:S(2)}) copy-start(bf16[4,529,192]{1,2,0:T(8,128)(2,1)} %get-tuple-element.109) | copy-start | bytes 2437636
  618.9 12.0 %copy-start.16 = (f32[4,529]{1,0:T(4,128)S(1)}, f32[4,529]{1,0:T(4,128)}, u32[]{:S(2)}) copy-start(f32[4,529]{1,0:T(4,128)} %copy-done.15) | copy-start | bytes 25396
  618.9 12.0 %copy-start.18 = (f32[4,529]{1,0:T(4,128)S(1)}, f32[4,529]{1,0:T(4,128)}, u32[]{:S(2)}) copy-start(f32[4,529]{1,0:T(4,128)} %copy-done.17) | copy-start | bytes 25396
  618.9 12.0 %copy-start.20 = (f32[768]{0:T(1024)S(1)}, f32[768]{0:T(1024)}, u32[]{:S(2)}) copy-start(f32[768]{0:T(1024)} %param.22) | copy-start | bytes 9220
  618.9 12.0 %copy-start.27 = (f32[768]{0:T(1024)S(1)}, f32[768]{0:T(1024)}, u32[]{:S(2)}) copy-start(f32[768]{0:T(1024)} %param.23) | copy-start | bytes 9220
  618.9 527.5 %reduce-scatter.10.cloned.1.call-start = ((), (), s32[]{:S(2)}) async-start(), calls=%async_computation.7 | async-start | bytes 2654208 | tf_op jit(solution)/shard_map/reduce_scatter | solution.py:167
  627.9 565.0 %reduce-scatter.8.cloned.1.call-start = ((), (), s32[]{:S(2)}) async-start(), calls=%async_computation.6 | async-start | bytes 2654208 | tf_op jit(solution)/shard_map/reduce_scatter | solution.py:163
  630.9 423.4 %copy-start.23 = (f32[768]{0:T(1024)S(1)}, f32[768]{0:T(1024)}, u32[]{:S(2)}) copy-start(f32[768]{0:T(1024)} %param.33) | copy-start | bytes 9220
  1054.4 8.9 copy-start.5
  1095.6 97.2 %copy-start.1 = (bf16[768,768]{1,0:T(8,128)(2,1)S(1)}, bf16[768,768]{1,0:T(8,128)(2,1)}, u32[]{:S(2)}) copy-start(bf16[768,768]{1,0:T(8,128)(2,1)} %param.32) | copy-start | bytes 3538948
  (14 other events, 55.7 us)
Sparse Core Ops, SparseCore 0:
  45.5 235.0 all-reduce.13
  305.1 231.3 all-reduce.15
  559.7 33.9 reduce-scatter.13
  609.5 444.7 all-reduce.17
  1058.1 41.5 reduce-scatter.11
  1103.9 42.4 reduce-scatter.9
  1150.4 42.4 reduce-scatter.7
where the time goes:
time: 1210 us; the launch traced here: 1200 us
  waiting for transfers between devices  954 us (79%)
  matrix products  103 us (9%)
  other arithmetic  50.7 us (4%)
  local copies, waits for them, and re-layouts  48.7 us (4%)
  blocking collectives  24.7 us (2%)
  between operations  16.1 us (1%)
    psum x1, waiting for transfers between devices, shards(): feedforward = lax.psum(partial_ff, 'mp')  414 us
    psum x1, waiting for transfers between devices, shards(): attention = lax.psum(partial_attn, 'mp')  235 us
    psum x1, waiting for transfers between devices, shards(): normed2_grad = lax.psum(partial_norm2, 'mp')  221 us
    reduce_scatter x1, waiting for transfers between devices, shards(): lax.psum_scatter(w_qkv_grad, 'dp', scatter_dimension=0, tiled=True)  46.4 us
    reduce_scatter x1, waiting for transfers between devices, shards(): lax.psum_scatter(w_up_grad, 'dp', scatter_dimension=0, tiled=True)  37.9 us
    unnamed x1, blocking collectives  24.7 us
  transfers between devices with their start and end apart: 7, of which 5 were waited for; matrix products, arithmetic and copies ran while one was open for 10% of the time, Pallas kernels for 0%

commit v1 on v0

--- a/solution.py
+++ b/solution.py
@@ -1,17 +1,546 @@
+import functools
 import jax
 import jax.numpy as jnp
 from jax import lax
+from jax.experimental import pallas as pl
+from jax.experimental.pallas import tpu as pltpu
 from jax.sharding import PartitionSpec as P
 
+MESH = pl.DeviceIdType.MESH
+BF = jnp.bfloat16
+F32 = jnp.float32
 HD = 64
-
-
-epsilon = 1e-06
+LANES = 128
+EPS = 1e-6
+MASKED = -1e30
+GELU_A = 0.7978845608028654
+GELU_B = 0.044715
+
+NN = (((1,), (0,)), ((), ()))
+NT = (((1,), (1,)), ((), ()))
+TN = (((0,), (0,)), ((), ()))
+
+
+def dot(a, b, dims):
+    return lax.dot_general(a, b, dims, preferred_element_type=F32)
+
+
+def place():
+    d = lax.axis_index("dp")
+    m = lax.axis_index("mp")
+    y, x, c = d // 4, (d // 2) % 2, d % 2
+    px = d + 2 - 4 * x
+    py = d + 4 - 8 * y
+    pc = d + 1 - 2 * c
+    return d, m, y, x, c, px, py, pc
+
+
+def other_z(m, k):
+    low = (m % 2 + k % 2) % 2
+    high = (m // 2 + k // 2) % 2
+    return 2 * high + low
+
+
+def enter(d, m, px, py, pc):
+    barrier = pltpu.get_barrier_semaphore()
+    for peer in ((px, m), (py, m), (pc, m)):
+        pl.semaphore_signal(barrier, inc=1, device_id=peer, device_id_type=MESH)
+    for k in (1, 2, 3):
+        pl.semaphore_signal(barrier, inc=1, device_id=(d, other_z(m, k)), device_id_type=MESH)
+    pl.semaphore_wait(barrier, 6)
+
+
+def forward_kernel(
+    fill_ref,
+    x_ref,
+    wa_in,
+    wu_in,
+    wd_in,
+    bias_in,
+    vec_ref,
+    layer_out,
+    qa_out,
+    k_out,
+    v_out,
+    ho_out,
+    n1_out,
+    n2_out,
+    r1_out,
+    hid_out,
+    gp_out,
+    wa_out,
+    wu_out,
+    wd_out,
+    wa,
+    wu,
+    wd,
+    bias,
+    q_s,
+    k_s,
+    v_s,
+    ho_s,
+    n1_s,
+    n2_s,
+    qa_s,
+    r1_s,
+    acc,
+    hid_s,
+    gp_s,
+    lo_s,
+    zs,
+    zr,
+    s1s,
+    s1r,
+    s2s,
+    s2r,
+    cs,
+    cr,
+    bs,
+    br,
+    load,
+    out,
+):
+    d, m, y, x, c, px, py, pc = place()
+    rows = x_ref.shape[0]
+    half = rows // 2
+    shards = (wa_in, wu_in, wd_in)
+
+    def part(w, mk, ys, xs, core, start, size):
+        if w == 0:
+            return wa.at[ys, xs, pl.ds(mk * 192 + core * 96 + start, size)]
+        full = wu if w == 1 else wd
+        return full.at[mk, ys, xs, pl.ds(core * 96 + start, size)]
+
+    every = slice(None)
+
+    def remote(src, dst, send, recv, peer):
+        return pltpu.make_async_remote_copy(
+            src_ref=src, dst_ref=dst, send_sem=send, recv_sem=recv, device_id=peer, device_id_type=MESH
+        )
+
+    def z_copy(w, k):
+        src = shards[w].at[y, x, pl.ds(c * 96, 96)]
+        return remote(src, part(w, m, y, x, c, 0, 96), zs.at[w, k - 1], zr.at[w, k - 1], (d, other_z(m, k)))
+
+    def z_wait(w, k):
+        here = part(w, other_z(m, k), y, x, c, 0, 96)
+        remote(here, here, zs.at[w, k - 1], zr.at[w, k - 1], (d, other_z(m, k))).wait_recv()
+
+    def s1(w, k, h):
+        mk = other_z(m, k)
+        here = part(w, mk, y, x, c, 48 * h, 48)
+        peer = (px, m) if h == 0 else (py, m)
+        return remote(here, here, s1s.at[w, k - 1, h], s1r.at[w, k - 1, h], peer)
+
+    def s1_wait(w, k, h):
+        mk = other_z(m, k)
+        here = part(w, mk, y, 1 - x, c, 0, 48) if h == 0 else part(w, mk, 1 - y, x, c, 48, 48)
+        peer = (px, m) if h == 0 else (py, m)
+        remote(here, here, s1s.at[w, k - 1, h], s1r.at[w, k - 1, h], peer).wait_recv()
+
+    def s2(w, k, h):
+        mk = other_z(m, k)
+        here = part(w, mk, y, every, c, 0, 48) if h == 0 else part(w, mk, every, x, c, 48, 48)
+        peer = (py, m) if h == 0 else (px, m)
+        return remote(here, here, s2s.at[w, k - 1, h], s2r.at[w, k - 1, h], peer)
+
+    def s2_wait(w, k, h):
+        mk = other_z(m, k)
+        here = part(w, mk, 1 - y, every, c, 0, 48) if h == 0 else part(w, mk, every, 1 - x, c, 48, 48)
+        peer = (py, m) if h == 0 else (px, m)
+        remote(here, here, s2s.at[w, k - 1, h], s2r.at[w, k - 1, h], peer).wait_recv()
+
+    def core(w, k):
+        here = part(w, other_z(m, k), every, every, c, 0, 96)
+        return remote(here, here, cs.at[w, k - 1], cr.at[w, k - 1], (pc, m))
+
+    def core_wait(w, k):
+        here = part(w, other_z(m, k), every, every, 1 - c, 0, 96)
+        remote(here, here, cs.at[w, k - 1], cr.at[w, k - 1], (pc, m)).wait_recv()
+
+    def go1(w, k):
+        z_wait(w, k)
+        s1(w, k, 0).start()
+        s1(w, k, 1).start()
+
+    def go2(w, k):
+        s1_wait(w, k, 0)
+        s1_wait(w, k, 1)
+        s2(w, k, 0).start()
+        s2(w, k, 1).start()
+
+    def go3(w, k):
+        s2_wait(w, k, 0)
+        s2_wait(w, k, 1)
+        core(w, k).start()
+
+    def own(w):
+        return pltpu.make_async_copy(shards[w], part(w, m, every, every, 0, 0, 192), load.at[w])
+
+    def bias_copy(k):
+        return remote(bias_in, bias.at[m], bs.at[k - 1], br.at[k - 1], (d, other_z(m, k)))
+
+    def bias_wait(k):
+        here = bias.at[other_z(m, k)]
+        remote(here, here, bs.at[k - 1], br.at[k - 1], (d, other_z(m, k))).wait_recv()
+
+    enter(d, m, px, py, pc)
+    for k in (1, 2, 3):
+        z_copy(0, k).start()
+    for k in (1, 2, 3):
+        bias_copy(k).start()
+    for w in range(3):
+        own(w).start()
+    own_bias = pltpu.make_async_copy(bias_in, bias.at[m], load.at[3])
+    own_bias.start()
+
+    def norm(values, gain, shift):
+        center = values - jnp.mean(values, axis=-1, keepdims=True)
+        inverse = lax.rsqrt(jnp.mean(center * center, axis=-1, keepdims=True) + EPS)
+        return center * inverse * gain + shift
+
+    n1_s[...] = norm(x_ref[...].astype(F32), vec_ref[0:1], vec_ref[1:2]).astype(BF)
+    save = [pltpu.make_async_copy(n1_s, n1_out, out.at[0])]
+    save[0].start()
+
+    go1(0, 1)
+    go2(0, 1)
+    go1(0, 2)
+    go1(0, 3)
+    for k in (1, 2, 3):
+        z_copy(1, k).start()
+    go3(0, 1)
+    go2(0, 2)
+    go2(0, 3)
+    for w in range(3):
+        own(w).wait()
+    own_bias.wait()
+    for k in (1, 2, 3):
+        bias_wait(k)
+    core_wait(0, 1)
+
+    group0 = m // 2
+    key_row = lax.broadcasted_iota(jnp.int32, (rows, LANES), 0)
+    lane = lax.broadcasted_iota(jnp.int32, (rows, LANES), 1)
+    mask_add = jnp.where(key_row < fill_ref[0], 0.0, MASKED)
+    lane_half = lax.broadcasted_iota(jnp.int32, (half, LANES), 1)
+
+    def project(g):
+        rows_w = pl.ds(pl.multiple_of(g * 384, 128), 384)
+        lanes = rows_w
+        qb = bias[0, 1:2, lanes] + bias[1, 1:2, lanes] + bias[2, 1:2, lanes] + bias[3, 1:2, lanes]
+        vb = bias[0, 2:3, lanes] + bias[1, 2:3, lanes] + bias[2, 2:3, lanes] + bias[3, 2:3, lanes]
+        n1 = n1_s[...]
+        q_s[:, lanes] = ((dot(n1, wa[0, 0, rows_w], NT) + qb) * (HD**-0.5)).astype(BF)
+        k_s[:, lanes] = dot(n1, wa[0, 1, rows_w], NT).astype(BF)
+        v_s[:, lanes] = (dot(n1, wa[1, 0, rows_w], NT) + vb).astype(BF)
+
+    def attend(p):
+        lanes = pl.ds(pl.multiple_of(p * LANES, LANES), LANES)
+        kp = k_s[:, lanes].astype(F32)
+        vp = v_s[:, lanes]
+        keys = []
+        for h in (0, 1):
+            own_lane = (lane < HD) if h == 0 else (lane >= HD)
+            first = HD if h == 0 else 0
+            extra = jnp.where(lane == first, mask_add, jnp.where(lane < first + 4, 1.0, 0.0))
+            keys.append(jnp.where(own_lane, kp, extra).astype(BF))
+        for b in (0, 1):
+            block = pl.ds(b * half, half)
+            qp = q_s[block, lanes].astype(F32)
+            mixed = []
+            for h in (0, 1):
+                own_lane = (lane_half < HD) if h == 0 else (lane_half >= HD)
+                first = HD if h == 0 else 0
+                base = jnp.where(own_lane, qp, jnp.where(lane_half == first, 1.0, 0.0))
+                s = dot(base.astype(BF), keys[h], NT)
+                peak = jnp.max(s, axis=-1, keepdims=True)
+                e = jnp.exp(s - peak)
+                total = jnp.sum(e, axis=-1, keepdims=True)
+                mixed.append(dot(e.astype(BF), vp, NN) / total)
+                lse = peak + jnp.log(total)
+                hi = lse.astype(BF).astype(F32)
+                lo = (lse - hi).astype(BF).astype(F32)
+                rest = lse - hi - lo
+                extra = jnp.where(
+                    lane_half == first + 1, -hi, jnp.where(lane_half == first + 2, -lo, jnp.where(lane_half == first + 3, -rest, 0.0))
+                )
+                extra = jnp.where(lane_half == first, 1.0, extra)
+                qa_s[2 * p + h, block] = jnp.where(own_lane, qp, extra).astype(BF)
+            ho_s[block, lanes] = jnp.where(lane_half < HD, mixed[0], mixed[1]).astype(BF)
+
+    project(group0)
+    go3(0, 2)
+    go3(0, 3)
+
+    def first_group(j, carry):
+        attend(group0 * 3 + j)
+        go1(1, j + 1)
+        return carry
+
+    lax.fori_loop(0, 3, first_group, 0)
+    for k in (1, 2, 3):
+        z_copy(2, k).start()
+    for k in (1, 2, 3):
+        go2(1, k)
+    core_wait(0, 2)
+    core_wait(0, 3)
+    project(1 - group0)
+
+    def second_group(j, carry):
+        attend((1 - group0) * 3 + j)
+        go3(1, j + 1)
+        go1(2, j + 1)
+        return carry
+
+    lax.fori_loop(0, 3, second_group, 0)
+    for k in (1, 2, 3):
+        go2(2, k)
+    pairs = ((qa_s, qa_out), (k_s, k_out), (v_s, v_out), (ho_s, ho_out))
+    for i, (a, b) in enumerate(pairs):
+        save.append(pltpu.make_async_copy(a, b, out.at[1 + i]))
+        save[-1].start()
+    r1 = x_ref[...].astype(F32) + dot(ho_s[...], wa[1, 1], NN) + vec_ref[2:3]
+    r1_s[...] = r1
+    n2_s[...] = norm(r1, vec_ref[3:4], vec_ref[4:5]).astype(BF)
+    acc[...] = r1 + vec_ref[5:6]
+    more = ((r1_s, r1_out), (n2_s, n2_out), (wa, wa_out))
+    for i, (a, b) in enumerate(more):
+        save.append(pltpu.make_async_copy(a, b, out.at[5 + i]))
+        save[-1].start()
+    for k in (1, 2, 3):
+        go3(2, k)
+
+    def feed(k, carry):
+        mk = other_z(m, k)
+
+        @pl.when(k > 0)
+        def _():
+            core_wait(1, k)
+            core_wait(2, k)
+
+        def up(n, inner):
+            cols = pl.ds(pl.multiple_of(n * 256, 256), 256)
+            w = wu[mk, :, :, :, cols].reshape(768, 256)
+            v = dot(n2_s[...], w, NN) + bias[mk, 0:1, cols]
+            sq = v * v
+            t = jnp.tanh(v * (GELU_A + GELU_A * GELU_B * sq))
+            hid_s[mk, :, cols] = (0.5 * v * (1.0 + t)).astype(BF)
+            slope = 0.5 * (1.0 + t) + 0.5 * v * (1.0 - t * t) * (GELU_A + 3.0 * GELU_A * GELU_B * sq)
+            gp_s[mk, :, cols] = slope.astype(BF)
+            return inner
+
+        lax.fori_loop(0, 3, up, 0)
+
+        def down(n, inner):
+            cols = pl.ds(pl.multiple_of(n * 256, 256), 256)
+            w = wd[mk, :, :, :, cols].reshape(768, 256)
+            acc[:, cols] += dot(hid_s[mk], w, NN)
+            return inner
+
+        lax.fori_loop(0, 3, down, 0)
+        return carry
+
+    lax.fori_loop(0, 4, feed, 0)
+    lo_s[...] = acc[...].astype(BF)
+    last = ((hid_s, hid_out), (gp_s, gp_out), (wu, wu_out), (wd, wd_out), (lo_s, layer_out))
+    for i, (a, b) in enumerate(last):
+        save.append(pltpu.make_async_copy(a, b, out.at[8 + i]))
+        save[-1].start()
+    for one in save:
+        one.wait()
+    for k in (1, 2, 3):
+        bias_copy(k).wait_send()
+    for w in range(3):
+        for k in (1, 2, 3):
+            z_copy(w, k).wait_send()
+            for h in (0, 1):
+                s1(w, k, h).wait_send()
+                s2(w, k, h).wait_send()
+            core(w, k).wait_send()
+
+
+def forward_call(fill, x, wa, wu, wd, bias, vec):
+    rows, width = x.shape
+    any_spec = pl.BlockSpec(memory_space=pl.ANY)
+    vmem = pl.BlockSpec(memory_space=pltpu.VMEM)
+    flat = (rows, width)
+
+    def hbm(shape, kind=BF):
+        return jax.ShapeDtypeStruct(shape, kind)
+
+    outs = [
+        hbm(flat),
+        hbm((12, rows, LANES)),
+        hbm(flat),
+        hbm(flat),
+        hbm(flat),
+        hbm(flat),
+        hbm(flat),
+        hbm(flat, F32),
+        hbm((4, rows, 768)),
+        hbm((4, rows, 768)),
+        hbm((2, 2, 768, 768)),
+        hbm((4, 2, 2, 192, 768)),
+        hbm((4, 2, 2, 192, 768)),
+    ]
+    dma = pltpu.SemaphoreType.DMA
+    scratch = [
+        pltpu.VMEM((2, 2, 768, 768), BF),
+        pltpu.VMEM((4, 2, 2, 192, 768), BF),
+        pltpu.VMEM((4, 2, 2, 192, 768), BF),
+        pltpu.VMEM((4, 8, 768), F32),
+        pltpu.VMEM(flat, BF),
+        pltpu.VMEM(flat, BF),
+        pltpu.VMEM(flat, BF),
+        pltpu.VMEM(flat, BF),
+        pltpu.VMEM(flat, BF),
+        pltpu.VMEM(flat, BF),
+        pltpu.VMEM((12, rows, LANES), BF),
+        pltpu.VMEM(flat, F32),
+        pltpu.VMEM(flat, F32),
+        pltpu.VMEM((4, rows, 768), BF),
+        pltpu.VMEM((4, rows, 768), BF),
+        pltpu.VMEM(flat, BF),
+        dma((3, 3)),
+        dma((3, 3)),
+        dma((3, 3, 2)),
+        dma((3, 3, 2)),
+        dma((3, 3, 2)),
+        dma((3, 3, 2)),
+        dma((3, 3)),
+        dma((3, 3)),
+        dma((3,)),
+        dma((3,)),
+        dma((4,)),
+        dma((13,)),
+    ]
+    return pl.pallas_call(
+        forward_kernel,
+        out_shape=outs,
+        in_specs=[pl.BlockSpec(memory_space=pltpu.SMEM), vmem, any_spec, any_spec, any_spec, any_spec, vmem],
+        out_specs=[any_spec] * len(outs),
+        scratch_shapes=scratch,
+        compiler_params=pltpu.CompilerParams(collective_id=0, has_side_effects=True, vmem_limit_bytes=60 << 20),
+        name="forward",
+    )(fill, x, wa, wu, wd, bias, vec)
+
+
+def prepare(patches, fill_lengths, cotangent, norm1_gain, norm1_shift, w_qkv, qv_bias, w_out, out_bias, norm2_gain, norm2_shift, w_up, up_bias, w_down, down_bias):
+    m = lax.axis_index("mp")
+    length, width = patches.shape[1:]
+    rows = -(-length // 32) * 32
+    pad = ((0, rows - length), (0, 0))
+    x = jnp.pad(lax.dynamic_index_in_dim(patches, m, 0, keepdims=False), pad)
+    cot = jnp.pad(lax.dynamic_index_in_dim(cotangent, m, 0, keepdims=False), pad)
+    fill = lax.dynamic_slice(fill_lengths, (m,), (1,))
+    wa = jnp.concatenate([jnp.transpose(w_qkv, (1, 2, 0)).reshape(576, width), w_out], axis=0)
+    wa = wa.reshape(2, 2, 192, width)
+    wu = w_up.reshape(2, 2, 192, width)
+    wd = w_down.reshape(2, 2, 192, width)
+    placed = lax.dynamic_update_slice(jnp.zeros((2, width), F32), qv_bias, (0, m * 192))
+    bias = jnp.concatenate([up_bias[None], placed, jnp.zeros((5, width), F32)], axis=0)
+    zero = jnp.zeros_like(norm1_gain)
+    vec = jnp.stack([norm1_gain, norm1_shift, out_bias, norm2_gain, norm2_shift, down_bias, zero, zero])
+    return x, cot, fill, wa, wu, wd, bias, vec
+
+
+def one_item(*args):
+    (patches, fill_lengths, cotangent, norm1_gain, norm1_shift, w_qkv, qv_bias, w_out, out_bias, norm2_gain, norm2_shift, w_up, up_bias, w_down, down_bias) = args
+    x, cot, fill, wa, wu, wd, bias, vec = prepare(*args)
+    length, width = patches.shape[1:]
+    lo, qa, k, v, ho, n1, n2, r1, hid, gp, waf, wuf, wdf = forward_call(fill, x, wa, wu, wd, bias, vec)
+    rows = x.shape[0]
+    layer_out = lax.all_gather(lo[:length], "mp", axis=0)
+    wdf = wdf.reshape(3072, width)
+    wuf = wuf.reshape(4, width, 768)
+    waf = waf.reshape(4, 768, width)
+    G = cot
+    hid2 = jnp.transpose(hid, (1, 0, 2)).reshape(rows, 3072)
+    ein = functools.partial(jnp.einsum, preferred_element_type=F32)
+    gw_down = ein("rd,rf->df", G, hid2)
+    hg = ein("rd,fd->rf", G, wdf)
+    pg = (hg * jnp.transpose(gp, (1, 0, 2)).reshape(rows, 3072)).astype(BF)
+    gw_up = ein("rd,rf->df", n2, pg)
+    U2 = ein("rmf,mdf->rd", pg.reshape(rows, 4, 768), wuf)
+
+    def stats(vals):
+        c = vals - jnp.mean(vals, -1, keepdims=True)
+        r = lax.rsqrt(jnp.mean(c * c, -1, keepdims=True) + EPS)
+        return c * r, r
+
+    def back(U, n, r, g):
+        s = U * g
+        return r * (s - s.mean(-1, keepdims=True) - n * (s * n).mean(-1, keepdims=True))
+
+    nn2, rr2 = stats(r1)
+    r1g = G.astype(F32) + back(U2, nn2, rr2, norm2_gain)
+    R = r1g.astype(BF)
+    gw_out = ein("rd,rc->dc", R, ho)
+    dho = ein("rd,cd->rc", R, waf[3]).astype(BF)
+    lanes = jnp.arange(128)
+    dq, dk, dv = [], [], []
+    for h in range(12):
+        sl = slice(h * 64, h * 64 + 64)
+        first = 64 if h % 2 == 0 else 0
+        mine = slice(64 - first, 128 - first)
+        kk = k[:, sl]
+        mask = jnp.where(jnp.arange(rows) < fill[0], 0.0, MASKED)[None]
+        q = qa[h][:, mine]
+        lse = -(qa[h][:, first + 1 : first + 4].astype(F32).sum(-1, keepdims=True))
+        s = ein("qd,kd->qk", q, kk) + mask
+        p = jnp.exp(s - lse)
+        dO = dho[:, sl]
+        dv.append(ein("qk,qd->kd", p.astype(BF), dO))
+        dp = ein("qd,kd->qk", dO, v[:, sl])
+        D = jnp.sum(dO.astype(F32) * ho[:, sl].astype(F32), -1, keepdims=True)
+        ds = (p * (dp - D)).astype(BF)
+        dq.append(ein("qk,kd->qd", ds, kk))
+        dk.append(ein("qk,qd->kd", ds, q))
+    dq, dk, dv = [jnp.concatenate(t, -1).astype(BF) for t in (dq, dk, dv)]
+    dq = dq * jnp.asarray(0.125, BF)
+    gw_qkv = jnp.stack([ein("rd,rc->dc", n1, t) for t in (dq, dk, dv)], 1)
+    U1 = sum(ein("rc,cd->rd", t, waf[i]) for i, t in enumerate((dq, dk, dv)))
+    nn1, rr1 = stats(x.astype(F32))
+    pgrad = r1g + back(U1, nn1, rr1, norm1_gain)
+    patches_grad = lax.all_gather(pgrad[:length].astype(BF), "mp", axis=0).astype(F32)
+    scat = functools.partial(lax.psum_scatter, tiled=True)
+
+    def both(t, dim_dp, dim_mp):
+        t = scat(t, "mp", scatter_dimension=dim_mp)
+        return scat(t, "dp", scatter_dimension=dim_dp)
+
+    def vecsum(t):
+        return scat(lax.psum(t, "mp"), "dp", scatter_dimension=0)
+
+    g_qkv = both(gw_qkv, 0, 2)
+    g_out = both(gw_out, 0, 1).T
+    g_up = both(gw_up, 0, 1)
+    g_down = both(gw_down, 0, 1).T
+    qv = jnp.stack([dq.astype(F32).sum(0), dv.astype(F32).sum(0)])
+    qv = both(qv, 1, 1)
+    ub = both(pg.astype(F32).sum(0), 0, 0)
+    return (
+        layer_out,
+        patches_grad,
+        vecsum((U1 * nn1).sum(0)),
+        vecsum(U1.sum(0)),
+        g_qkv,
+        qv,
+        g_out,
+        vecsum(r1g.sum(0)),
+        vecsum((U2 * nn2).sum(0)),
+        vecsum(U2.sum(0)),
+        g_up,
+        ub,
+        g_down,
+        vecsum(G.astype(F32).sum(0)),
+    )
 
 
 def normalize(values, gain, shift):
     center = values - jnp.mean(values, axis=-1, keepdims=True)
-    inverse = lax.rsqrt(jnp.mean(center * center, axis=-1, keepdims=True) + epsilon)
+    inverse = lax.rsqrt(jnp.mean(center * center, axis=-1, keepdims=True) + EPS)
     unit = center * inverse
     return (unit, inverse, unit * gain + shift)
 
@@ -37,7 +566,7 @@
     return jnp.where(usable[None, None, :], scores, -1e30)
 
 
-def attend(operands):
+def attend_items(operands):
     query_rows, key_rows, value_rows, usable = operands
     scores = masked_scores(split_heads(query_rows), split_heads(key_rows), usable)
     peak = jnp.max(scores, axis=-1, keepdims=True)
@@ -53,7 +582,7 @@
     )
 
 
-def attend_back(operands):
+def attend_items_back(operands):
     query_rows, key_rows, value_rows, usable, logsum, upstream = operands
     queries = split_heads(query_rows)
     keyset = split_heads(key_rows)
@@ -104,7 +633,7 @@
     key_rows = projected[:, :, 1].astype(jnp.bfloat16)
     value_rows = (projected[:, :, 2] + qv_bias[1]).astype(jnp.bfloat16)
     usable = jnp.arange(seq_len, dtype=jnp.int32)[None, :] < fill_lengths[:, None]
-    heads_out, logsum = lax.map(attend, (queries, key_rows, value_rows, usable))
+    heads_out, logsum = lax.map(attend_items, (queries, key_rows, value_rows, usable))
     partial_attn = jnp.einsum("isc,cd->isd", heads_out, w_out, preferred_element_type=jnp.float32)
     attention = lax.psum(partial_attn, "mp")
     residual1 = inputs + attention + out_bias
@@ -138,7 +667,7 @@
         "isd,cd->isc", residual_low, w_out, preferred_element_type=jnp.float32
     ).astype(jnp.bfloat16)
     query_grad, key_grad, value_grad = lax.map(
-        attend_back, (queries, key_rows, value_rows, usable, logsum, heads_grad)
+        attend_items_back, (queries, key_rows, value_rows, usable, logsum, heads_grad)
     )
     query_scaled = query_grad * scaling
     proj_grad = jnp.stack([query_scaled, key_grad, value_grad], axis=2)
@@ -190,8 +719,9 @@
 
 
 def solution(mesh):
+    body = one_item if (mesh.shape['dp'], mesh.shape['mp']) == (8, 4) else shards
     return jax.shard_map(
-        shards,
+        body,
         mesh=mesh,
         in_specs=(
             P("dp", None, None),

time: 1210 us -> 1010 us (0.83)
  waiting for transfers between devices: 954 us -> 673 us
  Pallas kernels: 0 us -> 82.2 us
  other arithmetic: 50.7 us -> 17.9 us
  blocking collectives: 24.7 us -> 51.7 us
  local copies, waits for them, and re-layouts: 48.7 us -> 67.1 us
    psum x3 -> x0, waiting for transfers between devices: 870 us -> none  [the longest x1 414 us: shards(): feedforward = lax.psum(partial_ff, 'mp')]
    reduce_scatter x3 -> x6, waiting for transfers between devices: 84.3 us -> 461 us  [the longest x3 323 us: both(): t = scat(t, 'mp', scatter_dimension=dim_mp)]
    unnamed x8 -> x14, waiting for transfers between devices: 0.14 us -> 120 us
    all_gather x0 -> x2, waiting for transfers between devices: none -> 91.8 us  [the longest x1 61.4 us: one_item(): lax.all_gather(pgrad[:length].astype(BF), 'mp', axis=0).astype(F32)]
    pallas_call x0 -> x1, Pallas kernels: none -> 82.2 us  [forward_call(): pl.pallas_call(forward_kernel, out_shape=outs, in_specs=[pl.BlockSpec(mem...]
    unnamed x74 -> x88, local copies, waits for them, and re-layouts: 22.2 us -> 52.9 us
    reduce_sum x13 -> x21, other arithmetic: 29.8 us -> 8.26 us  [the longest x12 2.6 us: one_item(): lse = -qa[h][:, first + 1:first + 4].astype(F32).sum(-1, keepdims=True)]
    unnamed x1 -> x2, blocking collectives: 24.7 us -> 41.6 us
  transfers between devices with their start and end apart: 7 -> 11, of which waited for: 5 -> 10; matrix products, arithmetic and copies ran while one was open for 10% -> 14% of each run, Pallas kernels for 0% -> 0%
where the time goes in v1:
time: 1010 us; the launch traced here: 1000 us
  waiting for transfers between devices  673 us (67%)
  matrix products  94.3 us (9%)
  Pallas kernels  82.2 us (8%)
  local copies, waits for them, and re-layouts  67.1 us (7%)
  blocking collectives  51.7 us (5%)
  other arithmetic  17.9 us (2%)
  between operations  17.1 us (2%)
    reduce_scatter x3, waiting for transfers between devices, both(): t = scat(t, 'mp', scatter_dimension=dim_mp)  323 us
    reduce_scatter x3, waiting for transfers between devices, both(): return scat(t, 'dp', scatter_dimension=dim_dp)  138 us
    unnamed x14, waiting for transfers between devices  120 us
    pallas_call x1, Pallas kernels, forward_call(): pl.pallas_call(forward_kernel, out_shape=outs, in_specs=[pl.BlockSpec(mem...  82.2 us
    all_gather x1, waiting for transfers between devices, one_item(): lax.all_gather(pgrad[:length].astype(BF), 'mp', axis=0).astype(F32)  61.4 us
    unnamed x88, local copies, waits for them, and re-layouts  52.9 us
    unnamed x2, blocking collectives  41.6 us
    all_gather x1, waiting for transfers between devices, one_item(): layer_out = lax.all_gather(lo[:length], 'mp', axis=0)  30.4 us
  transfers between devices with their start and end apart: 11, of which 10 were waited for; matrix products, arithmetic and copies ran while one was open for 14% of the time, Pallas kernels for 0%

profile of v1, /device:TPU:0, one launch (start us, length us, event | category | flops | bytes accessed | tf_op | source)
XLA Modules:
  0.0 1004.4 jit_solution(14149206637034203817)
XLA Ops:
  8.5 7.4 constant_dynamic-slice_fusion.1
  20.5 82.2 %forward.1 = (bf16[544,768]{1,0:T(8,128)(2,1)}, bf16[12,544,128]{2,1,0:T(8,128)(2,1)}, bf16[544,768]{1,0:T(8,128)(2,1)}, bf16[544,768]{1,0:T(8,128)(2,1)}, bf16[...) custom-call(s32[1]{0:T(128)} %dynamic_slice.10.fill_ref, ...), custom_call_target="tpu_custom_call" | custom-call | tf_op jit(solution)/shard_map/forward/pallas_call | solution.py:418
  109.1 6.3 convert_reduce_fusion
  115.4 3.2 fusion.6
  190.3 3.3 pad_maximum_fusion
  193.6 11.2 %copy.46 = f32[768,3,768]{0,1,2:T(4,128)} copy(f32[768,3,768]{2,0,1:T(8,128)} %pad_maximum_fusion) | data formatting | bytes 14155776
  204.8 8.2 copy.59
  213.1 9.7 fusion.212
  225.4 6.4 fusion.112
  242.4 2.8 fusion.209
  249.0 86.4 %reduce-scatter.29.cloned.1.call-done = f32[192,2304]{1,0:T(8,128)} async-done(((f32[768,2304]{1,0:T(8,128)}), f32[192,2304]{1,0:T(8,128)}) %reduce-scatter.29.cloned.1.call-update) | async-done | bytes 1769488
  340.8 158.9 %reduce-scatter.21.cloned.1.call-done = f32[768,768]{1,0:T(8,128)} async-done(((f32[768,3072]{1,0:T(8,128)}), f32[768,768]{1,0:T(8,128)}) %reduce-scatter.21.cloned.1.call-update) | async-done | bytes 2359312 | tf_op jit(solution)/shard_map/reduce_scatter | solution.py:510
  499.7 164.3 %reduce-scatter.25.cloned.1.call-done = f32[768,768]{1,0:T(8,128)} async-done(((f32[768,3072]{1,0:T(8,128)}), f32[768,768]{1,0:T(8,128)}) %reduce-scatter.25.cloned.1.call-update) | async-done | bytes 2359312 | tf_op jit(solution)/shard_map/reduce_scatter | solution.py:510
  667.2 18.3 %all-reduce.8 = f32[3072]{0:T(1024)S(1)} all-reduce(f32[3072]{0:T(1024)S(1)} %get-tuple-element.137), channel_id=17, replica_groups=mesh['dp'=8,'mp'=4] {'mp'}, use_global_device_ids=true, to_apply=%region_58.59.clone | all-reduce | flops 3072 | bytes 24576
  688.8 23.4 %all-reduce.11 = (f32[768]{0:T(1024)S(1)}, f32[768]{0:T(1024)S(1)}, f32[2,192]{1,0:T(2,128)S(1)}, f32[768]{0:T(1024)S(1)}, f32[768]{0:T(1024)S(1)}, /*index=5*/f...) all-reduce(f32[768]{0:T(1024)S(1)} %get-tuple-element.87, ...), channel_id=4, replica_groups=mesh['dp'=8,'mp'=4] {'dp'}, use_global_device_ids=true, to_apply=%region_34.35.clone | all-reduce | flops 5760 | bytes 46080
  713.2 10.1 %all-reduce.12 = (f32[96]{0:T(128)}, f32[96]{0:T(128)}, f32[96]{0:T(128)}, f32[96]{0:T(128)}, f32[96]{0:T(128)}, /*index=5*/f32[96]{0:T(128)}) all-reduce(f32[96]{0:T(128)S(1)} %dynamic-slice.1, f32[96]{0:T(128)S(1)} %dynamic-slice.3, f32[96]{0:T(128)S(1)} %dynamic-slice.7, ...), channel_id=1, replica_groups=mesh['dp'=8,'mp'=4] {'mp'}, use_global_device_ids=true, to_apply=%region_33.34 | all-reduce | flops 576 | bytes 4608 | tf_op jit(solution)/shard_map/psum | solution.py:514
  723.9 30.4 %all-gather.7.cloned.1.call-done = bf16[4,529,768]{2,1,0:T(8,128)(2,1)} async-done(((bf16[1,529,768]{2,1,0:T(8,128)(2,1)}), bf16[4,529,768]{2,1,0:T(8,128)(2,1)}) %all-gather.7.cloned.1.call-update) | async-done | bytes 3250192 | tf_op jit(solution)/shard_map/all_gather | solution.py:454
  754.3 4.9 copy.44
  759.2 61.4 %all-gather.9.cloned.1.call-done = bf16[4,529,768]{2,1,0:T(8,128)(2,1)} async-done(((bf16[1,529,768]{2,1,0:T(8,128)(2,1)}), bf16[4,529,768]{2,1,0:T(8,128)(2,1)}) %all-gather.9.cloned.1.call-update) | async-done | bytes 3250192 | tf_op jit(solution)/shard_map/all_gather | solution.py:506
  820.6 6.0 copy.45
  826.5 31.1 %reduce-scatter.33.cloned.1.call-done = f32[96,192]{1,0:T(8,128)} async-done(((f32[768,192]{1,0:T(8,128)}), f32[96,192]{1,0:T(8,128)}) %reduce-scatter.33.cloned.1.call-update) | async-done | bytes 73744
  859.3 45.2 %reduce-scatter.17.cloned.1.call-done = f32[96,3,192]{2,0,1:T(8,128)} async-done(((f32[768,3,192]{2,0,1:T(8,128)}), f32[96,3,192]{2,0,1:T(8,128)}) %reduce-scatter.17.cloned.1.call-update) | async-done | bytes 221200 | tf_op jit(solution)/shard_map/reduce_scatter | solution.py:511
  904.5 46.3 %reduce-scatter.23.cloned.1.call-done = f32[96,768]{1,0:T(8,128)} async-done(((f32[768,768]{1,0:T(8,128)}), f32[96,768]{1,0:T(8,128)}) %reduce-scatter.23.cloned.1.call-update) | async-done | bytes 294928 | tf_op jit(solution)/shard_map/reduce_scatter | solution.py:511
  950.8 46.8 %reduce-scatter.27.cloned.1.call-done = f32[96,768]{1,0:T(8,128)} async-done(((f32[768,768]{1,0:T(8,128)}), f32[96,768]{1,0:T(8,128)}) %reduce-scatter.27.cloned.1.call-update) | async-done | bytes 294928 | tf_op jit(solution)/shard_map/reduce_scatter | solution.py:511
  (243 shorter events, 113.2 us)
Async XLA Ops:
  7.2 239.6 %reduce-scatter.19.cloned.1.call-start = ((), (), s32[]{:S(2)}) async-start(), calls=%async_computation.10 | async-start | bytes 2949120 | tf_op jit(solution)/shard_map/reduce_scatter | solution.py:510
  102.7 1.9 copy-start.2
  108.9 6.5 slice-start
  109.0 9.6 copy-start.7
  109.0 6.4 slice-start.1
  115.4 3.3 copy-start.10
  118.7 2.0 copy-start.6
  123.2 212.2 %reduce-scatter.29.cloned.1.call-start = ((), (), s32[]{:S(2)}) async-start(), calls=%async_computation.17 | async-start | bytes 8847360
  126.8 22.8 %copy-start = (bf16[544,768]{1,0:T(8,128)(2,1)}, bf16[544,768]{1,0:T(8,128)(2,1)S(1)}, u32[]{:S(2)}) copy-start(bf16[544,768]{1,0:T(8,128)(2,1)S(1)} %convolution_convert_fusion) | copy-start | bytes 2506756
  182.0 7.1 copy-start.12
  182.4 5.6 copy-start.19
  213.1 286.6 %reduce-scatter.21.cloned.1.call-start = ((), (), s32[]{:S(2)}) async-start(), calls=%async_computation.11 | async-start | bytes 11796480 | tf_op jit(solution)/shard_map/reduce_scatter | solution.py:510
  222.9 441.2 %reduce-scatter.25.cloned.1.call-start = ((), (), s32[]{:S(2)}) async-start(), calls=%async_computation.13 | async-start | bytes 11796480 | tf_op jit(solution)/shard_map/reduce_scatter | solution.py:510
  222.9 2.5 copy-start.8
  231.8 456.1 %reduce-scatter.31.cloned.1.call-start = ((), (), s32[]{:S(2)}) async-start(), calls=%async_computation.18 | async-start | bytes 491520
  234.3 520.0 %all-gather.7.cloned.1.call-start = ((), (), s32[]{:S(2)}) async-start(), calls=%async_computation.15 | async-start | bytes 4116480 | tf_op jit(solution)/shard_map/all_gather | solution.py:454
  236.5 584.1 %all-gather.9.cloned.1.call-start = ((), (), s32[]{:S(2)}) async-start(), calls=%async_computation.16 | async-start | bytes 4116480 | tf_op jit(solution)/shard_map/all_gather | solution.py:506
  238.0 2.2 copy-start.20
  246.7 611.0 %reduce-scatter.33.cloned.1.call-start = ((), (), s32[]{:S(2)}) async-start(), calls=%async_computation.19 | async-start | bytes 884736
  249.0 655.5 %reduce-scatter.17.cloned.1.call-start = ((), (), s32[]{:S(2)}) async-start(), calls=%async_computation.9 | async-start | bytes 2654208 | tf_op jit(solution)/shard_map/reduce_scatter | solution.py:511
  340.7 610.1 %reduce-scatter.23.cloned.1.call-start = ((), (), s32[]{:S(2)}) async-start(), calls=%async_computation.12 | async-start | bytes 2654208 | tf_op jit(solution)/shard_map/reduce_scatter | solution.py:511
  499.7 164.4 %copy-start.29 = (u32[32]{0:T(128)S(1)}, u32[32]{0:T(128)}, u32[]{:S(2)}) copy-start(u32[32]{0:T(128)} %constant.73) | copy-start | bytes 388
  499.7 165.0 %copy-start.28 = (u32[32]{0:T(128)S(1)}, u32[32]{0:T(128)}, u32[]{:S(2)}) copy-start(u32[32]{0:T(128)} %constant.49) | copy-start | bytes 388
  499.7 497.9 %reduce-scatter.27.cloned.1.call-start = ((), (), s32[]{:S(2)}) async-start(), calls=%async_computation.14 | async-start | bytes 2654208 | tf_op jit(solution)/shard_map/reduce_scatter | solution.py:511
  (19 other events, 21.9 us)
Sparse Core Ops, SparseCore 0:
  123.4 46.9 reduce-scatter.18
  213.2 122.2 reduce-scatter.28
  337.8 161.7 reduce-scatter.20
  501.9 162.1 reduce-scatter.24
  666.1 21.6 reduce-scatter.30
  689.9 64.3 all-gather.6
  756.0 64.5 all-gather.8
  824.0 33.5 reduce-scatter.32
  861.9 42.4 reduce-scatter.16
  908.2 42.4 reduce-scatter.22
  955.1 42.4 reduce-scatter.26

commit v2 on v1

--- a/solution.py
+++ b/solution.py
@@ -426,6 +426,573 @@
     )(fill, x, wa, wu, wd, bias, vec)
 
 
+def backward_kernel(
+    fill_ref,
+    vec_ref,
+    lo_in,
+    g_in,
+    x_in,
+    qa_in,
+    k_in,
+    v_in,
+    ho_in,
+    n1_in,
+    n2_in,
+    r1_in,
+    hid_in,
+    gp_in,
+    wa_in,
+    wu_in,
+    wd_in,
+    lo_all,
+    pg_all,
+    grads,
+    sums,
+    g_s,
+    x_s,
+    qa_s,
+    k_s,
+    v_s,
+    ho_s,
+    n1_s,
+    n2_s,
+    r1_s,
+    wa,
+    hid_b,
+    gp_b,
+    wu_b,
+    wd_b,
+    pre_s,
+    acc,
+    res_s,
+    dho_s,
+    dq_s,
+    dk_s,
+    dv_s,
+    unit,
+    rc,
+    rx,
+    ry,
+    rz,
+    vs0,
+    vs_r,
+    vs_z,
+    los,
+    lor,
+    pgs,
+    pgr,
+    cs,
+    cr,
+    s1s,
+    s1r,
+    s2s,
+    s2r,
+    zs,
+    zr,
+    vss,
+    vsr,
+    vzs,
+    vzr,
+    load,
+    chunk_load,
+    own_sem,
+):
+    d, m, y, x, c, px, py, pc = place()
+    rows = g_in.shape[0]
+    half = rows // 2
+    every = slice(None)
+
+    def remote(src, dst, send, recv, peer):
+        return pltpu.make_async_remote_copy(
+            src_ref=src, dst_ref=dst, send_sem=send, recv_sem=recv, device_id=peer, device_id_type=MESH
+        )
+
+    quarter = rows // 64 * 16
+    starts = [(i * quarter, quarter if i < 3 else rows - 3 * quarter) for i in range(4)]
+
+    class Line:
+        def __init__(self, own, full, send, recv):
+            self.own, self.full, self.send, self.recv = own, full, send, recv
+
+        def copy(self, up, dist, j, sending):
+            step = 1 if up else -1
+            begin, size = starts[j]
+            source = m - step * (dist - 1) if sending else m - step * dist
+            there = self.full.at[source, pl.ds(begin, size)]
+            here = self.own.at[pl.ds(begin, size)] if (sending and dist == 1) else there
+            i = 0 if up else 1
+            return remote(here, there, self.send.at[i, dist - 1, j], self.recv.at[i, dist - 1, j], (d, m + step if sending else m - step))
+
+        def sends(self, up, dist):
+            return ((m >= dist - 1) & (m <= 2)) if up else ((m <= 4 - dist) & (m >= 1))
+
+        def gets(self, up, dist):
+            return (m >= dist) if up else (m <= 3 - dist)
+
+        def begin(self):
+            for j in range(4):
+                for up in (True, False):
+                    @pl.when(self.sends(up, 1))
+                    def _(up=up, j=j):
+                        self.copy(up, 1, j, True).start()
+
+        def relay(self, dist, j):
+            for up in (True, False):
+                @pl.when(self.gets(up, dist))
+                def _(up=up):
+                    self.copy(up, dist, j, False).wait_recv()
+
+                if dist < 3:
+                    @pl.when(self.sends(up, dist + 1))
+                    def _(up=up):
+                        self.copy(up, dist + 1, j, True).start()
+
+        def finish(self):
+            for dist in (1, 2, 3):
+                for j in range(4):
+                    for up in (True, False):
+                        @pl.when(self.sends(up, dist))
+                        def _(up=up, dist=dist, j=j):
+                            self.copy(up, dist, j, True).wait_send()
+
+    def core_send(a, u):
+        return remote(unit.at[a, u, every, every, 1 - c], rc.at[a, u], cs.at[a, u], cr.at[a, u], (pc, m))
+
+    def s1(a, u, h):
+        if h == 0:
+            return remote(unit.at[a, u, every, 1 - x, c, pl.ds(0, 48)], rx.at[a, u, 0], s1s.at[a, u, 0], s1r.at[a, u, 0], (px, m))
+        return remote(unit.at[a, u, 1 - y, every, c, pl.ds(48, 48)], rx.at[a, u, 1], s1s.at[a, u, 1], s1r.at[a, u, 1], (py, m))
+
+    def s2(a, u, h):
+        if h == 0:
+            return remote(unit.at[a, u, 1 - y, x, c, pl.ds(0, 48)], ry.at[a, u, 0], s2s.at[a, u, 0], s2r.at[a, u, 0], (py, m))
+        return remote(unit.at[a, u, y, 1 - x, c, pl.ds(48, 48)], ry.at[a, u, 1], s2s.at[a, u, 1], s2r.at[a, u, 1], (px, m))
+
+    def z_send(a, u):
+        return remote(unit.at[a, u, y, x, c], rz.at[a, u - 1], zs.at[a, u - 1], zr.at[a, u - 1], (d, other_z(m, u)))
+
+    def go1(a, u):
+        core_send(a, u).wait_recv()
+        unit[a, u, :, :, c] = (unit[a, u, :, :, c].astype(F32) + rc[a, u].astype(F32)).astype(BF)
+        s1(a, u, 0).start()
+        s1(a, u, 1).start()
+
+    def go2(a, u):
+        s1(a, u, 0).wait_recv()
+        unit[a, u, :, x, c, 0:48] = (unit[a, u, :, x, c, 0:48].astype(F32) + rx[a, u, 0].astype(F32)).astype(BF)
+        s2(a, u, 0).start()
+        s1(a, u, 1).wait_recv()
+        unit[a, u, y, :, c, 48:96] = (unit[a, u, y, :, c, 48:96].astype(F32) + rx[a, u, 1].astype(F32)).astype(BF)
+        s2(a, u, 1).start()
+
+    def go3(a, u):
+        for h in (0, 1):
+            s2(a, u, h).wait_recv()
+            part = pl.ds(48 * h, 48)
+            unit[a, u, y, x, c, part] = (unit[a, u, y, x, c, part].astype(F32) + ry[a, u, h].astype(F32)).astype(BF)
+
+        @pl.when(u > 0)
+        def _():
+            z_send(a, u).start()
+
+    def go4(a):
+        total = unit[a, 0, y, x, c].astype(F32)
+        for k in (1, 2, 3):
+            z_send(a, k).wait_recv()
+            total = total + rz[a, k - 1].astype(F32)
+        grads[a] = total
+
+    def copies(i):
+        pairs = (
+            (g_in, g_s),
+            (n2_in, n2_s),
+            (r1_in, r1_s),
+            (ho_in, ho_s),
+            (wa_in, wa),
+            (qa_in, qa_s),
+            (k_in, k_s),
+            (v_in, v_s),
+            (n1_in, n1_s),
+            (x_in, x_s),
+        )
+        return pltpu.make_async_copy(pairs[i][0], pairs[i][1], load.at[i])
+
+    def chunk(k):
+        slot = k % 2
+        mk = other_z(m, 3 - k)
+        pairs = ((wd_in, wd_b), (gp_in, gp_b), (hid_in, hid_b), (wu_in, wu_b))
+        return [pltpu.make_async_copy(a.at[mk], b.at[slot], chunk_load.at[i, slot]) for i, (a, b) in enumerate(pairs)]
+
+    line_lo = Line(lo_in, lo_all, los, lor)
+    line_pg = Line(dho_s, pg_all, pgs, pgr)
+
+    copies(0).start()
+    for one in chunk(0):
+        one.start()
+    enter(d, m, px, py, pc)
+    line_lo.begin()
+    own_lo = pltpu.make_async_copy(lo_in, lo_all.at[m], own_sem.at[0])
+    own_lo.start()
+    for i in range(1, 10):
+        copies(i).start()
+    copies(0).wait()
+    copies(1).wait()
+    sums_row = jnp.zeros((1, 768), F32)
+    for i in range(vs0.shape[0]):
+        vs0[i : i + 1] = sums_row
+    acc[...] = jnp.zeros_like(acc)
+
+    def feed(k, carry):
+        slot = k % 2
+        u = 3 - k
+        mk = other_z(m, u)
+
+        @pl.when(k < 3)
+        def _():
+            for one in chunk(k + 1):
+                one.start()
+
+        for one in chunk(k):
+            one.wait()
+
+        def first(n, inner):
+            cols = pl.ds(pl.multiple_of(n * 256, 256), 256)
+            hg = dot(g_s[...], wd_b[slot, cols], NT)
+            low = (hg * gp_b[slot, :, cols].astype(F32)).astype(BF)
+            pre_s[:, cols] = low
+            vs0[pl.ds(8 + mk, 1), cols] = jnp.sum(low.astype(F32), axis=0, keepdims=True)
+            return inner
+
+        lax.fori_loop(0, 3, first, 0)
+
+        def second(n, inner):
+            cols = pl.ds(pl.multiple_of(n * 384, 128), 384)
+            unit[0, u, n] = dot(g_s[:, cols], hid_b[slot], TN).astype(BF).reshape(2, 2, 96, 768)
+            unit[1, u, n] = dot(n2_s[:, cols], pre_s[...], TN).astype(BF).reshape(2, 2, 96, 768)
+            return inner
+
+        lax.fori_loop(0, 2, second, 0)
+        core_send(0, u).start()
+        core_send(1, u).start()
+
+        def third(n, inner):
+            cols = pl.ds(pl.multiple_of(n * 256, 256), 256)
+            acc[:, cols] += dot(pre_s[...], wu_b[slot, cols], NT)
+            return inner
+
+        lax.fori_loop(0, 3, third, 0)
+        go1(0, u)
+        go1(1, u)
+        return carry
+
+    lax.fori_loop(0, 4, feed, 0)
+    for j in range(4):
+        line_lo.relay(1, j)
+
+    def norm_back(values, upstream, gain):
+        center = values - jnp.mean(values, axis=-1, keepdims=True)
+        inverse = lax.rsqrt(jnp.mean(center * center, axis=-1, keepdims=True) + EPS)
+        n = center * inverse
+        scaled = upstream * gain
+        result = inverse * (
+            scaled - jnp.mean(scaled, axis=-1, keepdims=True) - n * jnp.mean(scaled * n, axis=-1, keepdims=True)
+        )
+        gain_part = jnp.sum(upstream * n, axis=0, keepdims=True)
+        return result, gain_part, jnp.sum(upstream, axis=0, keepdims=True)
+
+    for i in (2, 3, 4):
+        copies(i).wait()
+
+    def second_norm(i, carry):
+        block = pl.ds(pl.multiple_of(i * 32, 32), 32)
+        upstream = acc[block]
+        through, gain_part, shift_part = norm_back(r1_s[block], upstream, vec_ref[3:4])
+        g = g_s[block].astype(F32)
+        res = g + through
+        r1_s[block] = res
+        res_s[block] = res.astype(BF)
+        parts = (gain_part, shift_part, jnp.sum(res, axis=0, keepdims=True), jnp.sum(g, axis=0, keepdims=True))
+        return tuple(a + b for a, b in zip(carry, parts))
+
+    zero = jnp.zeros((1, 768), F32)
+    n2g, n2s, ob, db = lax.fori_loop(0, rows // 32, second_norm, (zero, zero, zero, zero))
+    vs0[2:3] = ob
+    vs0[3:4] = n2g
+    vs0[4:5] = n2s
+    vs0[5:6] = db
+
+    def heads_grad(n, carry):
+        cols = pl.ds(pl.multiple_of(n * 256, 256), 256)
+        dho_s[:, cols] = dot(res_s[...], wa[1, 1, cols], NT).astype(BF)
+        return carry
+
+    lax.fori_loop(0, 3, heads_grad, 0)
+    for i in (5, 6, 7):
+        copies(i).wait()
+
+    key_row = lax.broadcasted_iota(jnp.int32, (rows, LANES), 0)
+    lane = lax.broadcasted_iota(jnp.int32, (rows, LANES), 1)
+    mask_add = jnp.where(key_row < fill_ref[0], 0.0, MASKED)
+    lane_half = lax.broadcasted_iota(jnp.int32, (half, LANES), 1)
+    lane_turned = lax.broadcasted_iota(jnp.int32, (LANES, rows), 0)
+
+    def attend(p):
+        lanes = pl.ds(pl.multiple_of(p * LANES, LANES), LANES)
+        kp = k_s[:, lanes].astype(F32)
+        vp = v_s[:, lanes].astype(F32)
+        dop = dho_s[:, lanes]
+        dof = dop.astype(F32)
+        both = dof * ho_s[:, lanes].astype(F32)
+        ups = []
+        for h in (0, 1):
+            own_lane = (lane < HD) if h == 0 else (lane >= HD)
+            first = HD if h == 0 else 0
+            center = jnp.sum(jnp.where(own_lane, both, 0.0), axis=-1, keepdims=True)
+            hi = center.astype(BF).astype(F32)
+            lo = (center - hi).astype(BF).astype(F32)
+            rest = center - hi - lo
+            extra = jnp.where(lane == first, -hi, jnp.where(lane == first + 1, -lo, jnp.where(lane == first + 2, -rest, 0.0)))
+            ups.append(jnp.where(own_lane, dof, extra).astype(BF))
+        turned = [None, None]
+        for b in (0, 1):
+            block = slice(b * half, (b + 1) * half)
+            dks, dvs = [], []
+            for h in (0, 1):
+                own_lane = (lane_half < HD) if h == 0 else (lane_half >= HD)
+                first = HD if h == 0 else 0
+                extra = jnp.where(lane_half == first, mask_add[block], jnp.where(lane_half < first + 4, 1.0, 0.0))
+                keys = jnp.where(own_lane, kp[block], extra).astype(BF)
+                values = jnp.where(own_lane, vp[block], jnp.where(lane_half < first + 3, 1.0, 0.0)).astype(BF)
+                qa = qa_s[2 * p + h]
+                probs = jnp.exp(dot(keys, qa, NT))
+                dvs.append(dot(probs.astype(BF), dop, NN))
+                ds = (probs * dot(values, ups[h], NT)).astype(BF)
+                dks.append(dot(ds, qa, NN))
+                t = dot(keys, ds, TN)
+                turned[h] = t if b == 0 else turned[h] + t
+            here = pl.ds(b * half, half)
+            dk_s[here, lanes] = jnp.where(lane_half < HD, dks[0], dks[1]).astype(BF)
+            dv_s[here, lanes] = jnp.where(lane_half < HD, dvs[0], dvs[1]).astype(BF)
+        dq = jnp.where(lane_turned < HD, turned[0], turned[1])
+        dq_s[:, lanes] = (jnp.transpose(dq) * (HD**-0.5)).astype(BF)
+
+    def pair(p, carry):
+        attend(p)
+
+        @pl.when(p < 4)
+        def _():
+            go2(0, 3 - p)
+            go2(1, 3 - p)
+
+        @pl.when(p >= 2)
+        def _():
+            go3(0, 5 - p)
+            go3(1, 5 - p)
+
+        for j in range(4):
+            @pl.when(p == j + 1)
+            def _(j=j):
+                line_lo.relay(2, j)
+
+        return carry
+
+    lax.fori_loop(0, 6, pair, 0)
+    vs0[6:7] = jnp.sum(dq_s[...].astype(F32), axis=0, keepdims=True)
+    vs0[7:8] = jnp.sum(dv_s[...].astype(F32), axis=0, keepdims=True)
+    copies(8).wait()
+    copies(9).wait()
+
+    def last_product(n, carry):
+        cols = pl.ds(pl.multiple_of(n * 256, 256), 256)
+        acc[:, cols] = (
+            dot(dq_s[...], wa[0, 0, :, cols], NN) + dot(dk_s[...], wa[0, 1, :, cols], NN) + dot(dv_s[...], wa[1, 0, :, cols], NN)
+        )
+        return carry
+
+    lax.fori_loop(0, 3, last_product, 0)
+
+    def first_norm(i, carry):
+        block = pl.ds(pl.multiple_of(i * 32, 32), 32)
+        through, gain_part, shift_part = norm_back(x_s[block].astype(F32), acc[block], vec_ref[0:1])
+        dho_s[block] = (r1_s[block] + through).astype(BF)
+        return tuple(a + b for a, b in zip(carry, (gain_part, shift_part)))
+
+    n1g, n1s = lax.fori_loop(0, rows // 32, first_norm, (zero, zero))
+    vs0[0:1] = n1g
+    vs0[1:2] = n1s
+    line_pg.begin()
+    own_pg = pltpu.make_async_copy(dho_s, pg_all.at[m], own_sem.at[1])
+    own_pg.start()
+
+    lane_tile = lax.broadcasted_iota(jnp.int32, (384, LANES), 1)
+
+    def turn(v):
+        return pltpu.roll(v, HD, 1)
+
+    def attention_grads(e, carry):
+        def tile(n, inner):
+            cols = pl.ds(pl.multiple_of(n * 384, 128), 384)
+            heads = pl.ds(pl.multiple_of(e * 384, 128), 384)
+            n1 = n1_s[:, cols]
+            q, k, v = [dot(n1, t[:, heads], TN) for t in (dq_s, dk_s, dv_s)]
+            o = dot(res_s[:, cols], ho_s[:, heads], TN)
+
+            def block(t, i):
+                return t[:, i * LANES : (i + 1) * LANES]
+
+            def low(a, b):
+                return jnp.where(lane_tile < HD, block(a, 1), turn(block(b, 1)))
+
+            def high(a, b):
+                return jnp.where(lane_tile < HD, turn(block(a, 1)), block(b, 1))
+
+            even = [block(q, 0), low(q, k), block(k, 0), block(v, 0), low(v, o), block(o, 0)]
+            odd = [high(q, k), block(q, 2), block(k, 2), high(v, o), block(v, 2), block(o, 2)]
+            ue, uo = other_z(m, 2 * e), other_z(m, 2 * e + 1)
+            for i in range(6):
+                lanes = slice(i * LANES, (i + 1) * LANES)
+                unit[2, ue, n, :, :, :, lanes] = even[i].astype(BF).reshape(2, 2, 96, LANES)
+                unit[2, uo, n, :, :, :, lanes] = odd[i].astype(BF).reshape(2, 2, 96, LANES)
+            return inner
+
+        lax.fori_loop(0, 2, tile, 0)
+        core_send(2, other_z(m, 2 * e)).start()
+        core_send(2, other_z(m, 2 * e + 1)).start()
+        return carry
+
+    lax.fori_loop(0, 2, attention_grads, 0)
+
+    def run(stage, start=3):
+        def body(i, carry):
+            stage(2, 3 - i)
+            return carry
+
+        lax.fori_loop(0, 4, body, 0)
+
+    run(go1)
+
+    peers = ((pc, m), (px, m), (py, m))
+
+    def small(i):
+        return remote(vs0, vs_r.at[i], vss.at[i], vsr.at[i], peers[i])
+
+    for i in range(3):
+        small(i).start()
+        small(i).wait()
+        vs0[...] += vs_r[i]
+
+    def small_z(k):
+        return remote(vs0, vs_z.at[k - 1], vzs.at[k - 1], vzr.at[k - 1], (d, other_z(m, k)))
+
+    for k in (1, 2, 3):
+        small_z(k).start()
+    run(go2)
+    run(go3)
+    for j in range(4):
+        line_pg.relay(1, j)
+    for j in range(4):
+        line_lo.relay(3, j)
+    for j in range(4):
+        line_pg.relay(2, j)
+    go4(0)
+    go4(1)
+    go4(2)
+    total = vs0[...]
+    for k in (1, 2, 3):
+        small_z(k).wait_recv()
+        total = total + vs_z[k - 1]
+    sums[...] = total
+    for j in range(4):
+        line_pg.relay(3, j)
+    line_lo.finish()
+    line_pg.finish()
+    own_lo.wait()
+    own_pg.wait()
+    for k in (1, 2, 3):
+        small_z(k).wait_send()
+    for a in range(3):
+        for u in range(4):
+            core_send(a, u).wait_send()
+            for h in (0, 1):
+                s1(a, u, h).wait_send()
+                s2(a, u, h).wait_send()
+            if u > 0:
+                z_send(a, u).wait_send()
+
+
+def backward_call(fill, vec, lo, g, x, qa, k, v, ho, n1, n2, r1, hid, gp, wa, wu, wd):
+    rows, width = x.shape
+    any_spec = pl.BlockSpec(memory_space=pl.ANY)
+    vmem = pl.BlockSpec(memory_space=pltpu.VMEM)
+    flat = (rows, width)
+    outs = [
+        jax.ShapeDtypeStruct((4, rows, width), BF),
+        jax.ShapeDtypeStruct((4, rows, width), BF),
+        jax.ShapeDtypeStruct((3, 96, 768), F32),
+        jax.ShapeDtypeStruct((16, width), F32),
+    ]
+    dma = pltpu.SemaphoreType.DMA
+    scratch = [
+        pltpu.VMEM(flat, BF),
+        pltpu.VMEM(flat, BF),
+        pltpu.VMEM((12, rows, LANES), BF),
+        pltpu.VMEM(flat, BF),
+        pltpu.VMEM(flat, BF),
+        pltpu.VMEM(flat, BF),
+        pltpu.VMEM(flat, BF),
+        pltpu.VMEM(flat, BF),
+        pltpu.VMEM(flat, F32),
+        pltpu.VMEM((2, 2, 768, 768), BF),
+        pltpu.VMEM((2, rows, 768), BF),
+        pltpu.VMEM((2, rows, 768), BF),
+        pltpu.VMEM((2, 768, 768), BF),
+        pltpu.VMEM((2, 768, 768), BF),
+        pltpu.VMEM(flat, BF),
+        pltpu.VMEM(flat, F32),
+        pltpu.VMEM(flat, BF),
+        pltpu.VMEM(flat, BF),
+        pltpu.VMEM(flat, BF),
+        pltpu.VMEM(flat, BF),
+        pltpu.VMEM(flat, BF),
+        pltpu.VMEM((3, 4, 2, 2, 2, 96, 768), BF),
+        pltpu.VMEM((3, 4, 2, 2, 96, 768), BF),
+        pltpu.VMEM((3, 4, 2, 2, 48, 768), BF),
+        pltpu.VMEM((3, 4, 2, 48, 768), BF),
+        pltpu.VMEM((3, 3, 96, 768), BF),
+        pltpu.VMEM((16, width), F32),
+        pltpu.VMEM((3, 16, width), F32),
+        pltpu.VMEM((3, 16, width), F32),
+        dma((2, 3, 4)),
+        dma((2, 3, 4)),
+        dma((2, 3, 4)),
+        dma((2, 3, 4)),
+        dma((3, 4)),
+        dma((3, 4)),
+        dma((3, 4, 2)),
+        dma((3, 4, 2)),
+        dma((3, 4, 2)),
+        dma((3, 4, 2)),
+        dma((3, 3)),
+        dma((3, 3)),
+        dma((3,)),
+        dma((3,)),
+        dma((3,)),
+        dma((3,)),
+        dma((10,)),
+        dma((4, 2)),
+        dma((2,)),
+    ]
+    return pl.pallas_call(
+        backward_kernel,
+        out_shape=outs,
+        in_specs=[pl.BlockSpec(memory_space=pltpu.SMEM), vmem] + [any_spec] * 15,
+        out_specs=[any_spec, any_spec, vmem, vmem],
+        scratch_shapes=scratch,
+        compiler_params=pltpu.CompilerParams(collective_id=1, has_side_effects=True, vmem_limit_bytes=62 << 20),
+        name="backward",
+    )(fill, vec, lo, g, x, qa, k, v, ho, n1, n2, r1, hid, gp, wa, wu, wd)
+
+
 def prepare(patches, fill_lengths, cotangent, norm1_gain, norm1_shift, w_qkv, qv_bias, w_out, out_bias, norm2_gain, norm2_shift, w_up, up_bias, w_down, down_bias):
     m = lax.axis_index("mp")
     length, width = patches.shape[1:]
@@ -446,95 +1013,47 @@
 
 
 def one_item(*args):
-    (patches, fill_lengths, cotangent, norm1_gain, norm1_shift, w_qkv, qv_bias, w_out, out_bias, norm2_gain, norm2_shift, w_up, up_bias, w_down, down_bias) = args
+    length, width = args[0].shape[1:]
     x, cot, fill, wa, wu, wd, bias, vec = prepare(*args)
-    length, width = patches.shape[1:]
-    lo, qa, k, v, ho, n1, n2, r1, hid, gp, waf, wuf, wdf = forward_call(fill, x, wa, wu, wd, bias, vec)
-    rows = x.shape[0]
-    layer_out = lax.all_gather(lo[:length], "mp", axis=0)
-    wdf = wdf.reshape(3072, width)
-    wuf = wuf.reshape(4, width, 768)
-    waf = waf.reshape(4, 768, width)
-    G = cot
-    hid2 = jnp.transpose(hid, (1, 0, 2)).reshape(rows, 3072)
-    ein = functools.partial(jnp.einsum, preferred_element_type=F32)
-    gw_down = ein("rd,rf->df", G, hid2)
-    hg = ein("rd,fd->rf", G, wdf)
-    pg = (hg * jnp.transpose(gp, (1, 0, 2)).reshape(rows, 3072)).astype(BF)
-    gw_up = ein("rd,rf->df", n2, pg)
-    U2 = ein("rmf,mdf->rd", pg.reshape(rows, 4, 768), wuf)
-
-    def stats(vals):
-        c = vals - jnp.mean(vals, -1, keepdims=True)
-        r = lax.rsqrt(jnp.mean(c * c, -1, keepdims=True) + EPS)
-        return c * r, r
-
-    def back(U, n, r, g):
-        s = U * g
-        return r * (s - s.mean(-1, keepdims=True) - n * (s * n).mean(-1, keepdims=True))
-
-    nn2, rr2 = stats(r1)
-    r1g = G.astype(F32) + back(U2, nn2, rr2, norm2_gain)
-    R = r1g.astype(BF)
-    gw_out = ein("rd,rc->dc", R, ho)
-    dho = ein("rd,cd->rc", R, waf[3]).astype(BF)
-    lanes = jnp.arange(128)
-    dq, dk, dv = [], [], []
-    for h in range(12):
-        sl = slice(h * 64, h * 64 + 64)
-        first = 64 if h % 2 == 0 else 0
-        mine = slice(64 - first, 128 - first)
-        kk = k[:, sl]
-        mask = jnp.where(jnp.arange(rows) < fill[0], 0.0, MASKED)[None]
-        q = qa[h][:, mine]
-        lse = -(qa[h][:, first + 1 : first + 4].astype(F32).sum(-1, keepdims=True))
-        s = ein("qd,kd->qk", q, kk) + mask
-        p = jnp.exp(s - lse)
-        dO = dho[:, sl]
-        dv.append(ein("qk,qd->kd", p.astype(BF), dO))
-        dp = ein("qd,kd->qk", dO, v[:, sl])
-        D = jnp.sum(dO.astype(F32) * ho[:, sl].astype(F32), -1, keepdims=True)
-        ds = (p * (dp - D)).astype(BF)
-        dq.append(ein("qk,kd->qd", ds, kk))
-        dk.append(ein("qk,qd->kd", ds, q))
-    dq, dk, dv = [jnp.concatenate(t, -1).astype(BF) for t in (dq, dk, dv)]
-    dq = dq * jnp.asarray(0.125, BF)
-    gw_qkv = jnp.stack([ein("rd,rc->dc", n1, t) for t in (dq, dk, dv)], 1)
-    U1 = sum(ein("rc,cd->rd", t, waf[i]) for i, t in enumerate((dq, dk, dv)))
-    nn1, rr1 = stats(x.astype(F32))
-    pgrad = r1g + back(U1, nn1, rr1, norm1_gain)
-    patches_grad = lax.all_gather(pgrad[:length].astype(BF), "mp", axis=0).astype(F32)
-    scat = functools.partial(lax.psum_scatter, tiled=True)
-
-    def both(t, dim_dp, dim_mp):
-        t = scat(t, "mp", scatter_dimension=dim_mp)
-        return scat(t, "dp", scatter_dimension=dim_dp)
-
-    def vecsum(t):
-        return scat(lax.psum(t, "mp"), "dp", scatter_dimension=0)
-
-    g_qkv = both(gw_qkv, 0, 2)
-    g_out = both(gw_out, 0, 1).T
-    g_up = both(gw_up, 0, 1)
-    g_down = both(gw_down, 0, 1).T
-    qv = jnp.stack([dq.astype(F32).sum(0), dv.astype(F32).sum(0)])
-    qv = both(qv, 1, 1)
-    ub = both(pg.astype(F32).sum(0), 0, 0)
+    lo, qa, k, v, ho, n1, n2, r1, hid, gp, wa, wu, wd = forward_call(fill, x, wa, wu, wd, bias, vec)
+    wu = wu.reshape(4, width, 768)
+    wd = wd.reshape(4, 768, width)
+    lo_all, pg_all, grads, sums = backward_call(fill, vec, lo, cot, x, qa, k, v, ho, n1, n2, r1, hid, gp, wa, wu, wd)
+    d = lax.axis_index("dp")
+    m = lax.axis_index("mp")
+    layer_out = lo_all[:, :length]
+    patches_grad = pg_all[:, :length].astype(F32)
+    g = grads[2]
+    is_even = m % 2 == 0
+
+    def pick(even, odd):
+        def join(parts):
+            return jnp.concatenate([g[:, a:b] for a, b in parts], axis=1)
+
+        return jnp.where(is_even, join(even), join(odd))
+
+    q_grad = pick([(0, 192)], [(0, 64), (128, 256)])
+    k_grad = pick([(256, 384), (192, 256)], [(64, 128), (256, 384)])
+    v_grad = pick([(384, 576)], [(384, 448), (512, 640)])
+    o_grad = pick([(640, 768), (576, 640)], [(448, 512), (640, 768)])
+    mine = lax.dynamic_slice(sums, (0, d * 96), (8, 96))
+    qv = lax.dynamic_slice(sums, (6, m * 192 + d * 24), (2, 24))
+    up_grad = lax.dynamic_slice(sums, (8 + m, d * 96), (1, 96))[0]
     return (
         layer_out,
         patches_grad,
-        vecsum((U1 * nn1).sum(0)),
-        vecsum(U1.sum(0)),
-        g_qkv,
+        mine[0],
+        mine[1],
+        jnp.stack([q_grad, k_grad, v_grad], axis=1),
         qv,
-        g_out,
-        vecsum(r1g.sum(0)),
-        vecsum((U2 * nn2).sum(0)),
-        vecsum(U2.sum(0)),
-        g_up,
-        ub,
-        g_down,
-        vecsum(G.astype(F32).sum(0)),
+        o_grad.T,
+        mine[2],
+        mine[3],
+        mine[4],
+        grads[1],
+        up_grad,
+        grads[0].T,
+        mine[5],
     )
 
 

time: 1010 us -> 276 us (0.27)
  waiting for transfers between devices: 673 us -> 0 us
  Pallas kernels: 82.2 us -> 238 us
  matrix products: 94.3 us -> 0 us
  blocking collectives: 51.7 us -> 0 us
  local copies, waits for them, and re-layouts: 67.1 us -> 32.2 us
  between operations: 17.1 us -> 0.78 us
  other arithmetic: 17.9 us -> 4.54 us
    reduce_scatter x6 -> x0, waiting for transfers between devices: 461 us -> none  [the longest x3 323 us: both(): t = scat(t, 'mp', scatter_dimension=dim_mp)]
    pallas_call x0 -> x1, Pallas kernels: none -> 156 us  [backward_call(): pl.pallas_call(backward_kernel, out_shape=outs, in_specs=[pl.BlockSpec(me...]
    unnamed x14 -> x0, waiting for transfers between devices: 120 us -> none
    dot_general x72 -> x0, matrix products: 94.3 us -> none  [the longest x12 16.6 us: one_item(): dp = ein('qd,kd->qk', dO, v[:, sl])]
    all_gather x2 -> x0, waiting for transfers between devices: 91.8 us -> none  [the longest x1 61.4 us: one_item(): lax.all_gather(pgrad[:length].astype(BF), 'mp', axis=0).astype(F32)]
    unnamed x88 -> x9, local copies, waits for them, and re-layouts: 52.9 us -> 9.21 us
    unnamed x2 -> x0, blocking collectives: 41.6 us -> none
  transfers between devices with their start and end apart: 11 -> 0, of which waited for: 10 -> 0; matrix products, arithmetic and copies ran while one was open for 14% -> 0% of each run, Pallas kernels for 0% -> 0%
where the time goes in v2:
time: 276 us; the launch traced here: 275 us
  Pallas kernels  238 us (86%)
  local copies, waits for them, and re-layouts  32.2 us (12%)
  other arithmetic  4.54 us (2%)
    pallas_call x1, Pallas kernels, backward_call(): pl.pallas_call(backward_kernel, out_shape=outs, in_specs=[pl.BlockSpec(me...  156 us
    pallas_call x1, Pallas kernels, forward_call(): pl.pallas_call(forward_kernel, out_shape=outs, in_specs=[pl.BlockSpec(mem...  82.1 us
    unnamed x9, local copies, waits for them, and re-layouts  9.21 us
    dynamic_slice x1, local copies, waits for them, and re-layouts, prepare(): lax.dynamic_index_in_dim(cotangent, m, 0, keepdims=False)  6.25 us

profile of v2, /device:TPU:0, one launch (start us, length us, event | category | flops | bytes accessed | tf_op | source)
XLA Modules:
  0.0 275.2 jit_solution(12663449529223627391)
XLA Ops:
  0.7 1.2 dynamic_slice.19.fill_ref
  2.0 0.7 stack.31
  2.7 0.7 stack.32
  3.4 0.7 stack.33
  4.1 0.7 stack.34
  4.7 0.7 stack.35
  5.4 0.7 broadcast_in_dim.6
  6.1 0.7 stack.36
  6.8 0.8 dynamic_update_slice.3
  8.9 2.4 pad_maximum_fusion
  11.3 6.3 %constant_dynamic-slice_fusion.1 = (bf16[1,529,768]{2,0,1:T(2,128)(2,1)S(1)}, bf16[1,529,768]{2,0,1:T(2,128)(2,1)S(1)}) fusion(bf16[4,529,768]{2,0,1:T(4,128)(2,1)} %param.17, s32[]{:T(128)S(6)} %select_n.55, bf16[4,529,768]{2,0,1:T(4,128)(2,1)} %param.15), kind=kLoop, calls=%fused_computation.20 | loop fusion | bytes 3250180 | tf_op jit(solution)/shard_map/jit(dynamic_index_in_dim)/dynamic_slice | solution.py:1002
  17.7 1.0 pad.8.g_in
  18.8 1.0 pad.7.x_ref.x_in
  19.8 82.1 %forward.1 = (bf16[544,768]{1,0:T(8,128)(2,1)}, bf16[12,544,128]{2,1,0:T(8,128)(2,1)}, bf16[544,768]{1,0:T(8,128)(2,1)}, bf16[544,768]{1,0:T(8,128)(2,1)}, bf16[...) custom-call(s32[1]{0:T(128)} %dynamic_slice.19.fill_ref, ...), custom_call_target="tpu_custom_call" | custom-call | tf_op jit(solution)/shard_map/forward/pallas_call | solution.py:418
  101.8 155.6 %backward.1 = (bf16[4,544,768]{2,1,0:T(8,128)(2,1)}, bf16[4,544,768]{2,1,0:T(8,128)(2,1)}, f32[3,96,768]{2,1,0:T(8,128)}, f32[16,768]{1,0:T(8,128)}) custom-call(s32[1]{0:T(128)} %dynamic_slice.19.fill_ref, f32[8,768]{1,0:T(8,128)} %stack.37.vec_ref, bf16[544,768]{1,0:T(8,128)(2,1)} %get-tuple-element.31.lo_in, bf16[544,768]{1,0:T(8,128)(2,1)} %pad.8.g_in, ...), custom_call_target="tpu_custom_call" | custom-call | tf_op jit(solution)/shard_map/backward/pallas_call | solution.py:985
  257.5 1.3 dynamic-slice_bitcast_fusion
  258.8 2.1 slice.71
  260.9 3.0 %copy.34 = bf16[4,529,768]{2,0,1:T(4,128)(2,1)} copy(bf16[4,529,768]{2,1,0:T(8,128)(2,1)S(1)} %slice.71) | data formatting | bytes 6500352
  263.9 1.5 constant_dynamic-slice_fusion.3
  265.3 0.8 constant_dynamic-slice_fusion
  266.7 0.9 slice_bitcast_fusion
  268.0 0.7 pad_maximum_fusion.1
  268.7 0.7 copy.36
  269.9 5.3 %copy.35 = f32[4,529,768]{2,0,1:T(4,128)} copy(f32[4,529,768]{2,1,0:T(8,128)S(1)} %slice_convert_fusion) | data formatting | bytes 13000704
  (19 shorter events, 3.1 us)
Async XLA Ops:
  260.9 5.8 %copy-start.1 = (f32[3,96,768]{2,1,0:T(8,128)S(1)}, f32[3,96,768]{2,1,0:T(8,128)}, u32[]{:S(2)}) copy-start(f32[3,96,768]{2,1,0:T(8,128)} %get-tuple-element.47) | copy-start | bytes 2654212
  263.9 5.6 %copy-start = (bf16[4,544,768]{2,1,0:T(8,128)(2,1)S(1)}, bf16[4,544,768]{2,1,0:T(8,128)(2,1)}, u32[]{:S(2)}) copy-start(bf16[4,544,768]{2,1,0:T(8,128)(2,1)} %get-tuple-element.45) | copy-start | bytes 10027012

commit v3 on v2

--- a/solution.py
+++ b/solution.py
@@ -53,11 +53,18 @@
 def forward_kernel(
     fill_ref,
     x_ref,
-    wa_in,
+    wq_in,
+    wo_in,
     wu_in,
     wd_in,
-    bias_in,
-    vec_ref,
+    qv_bias,
+    up_bias,
+    gain1,
+    shift1,
+    out_bias,
+    gain2,
+    shift2,
+    down_bias,
     layer_out,
     qa_out,
     k_out,
@@ -89,6 +96,7 @@
     lo_s,
     zs,
     zr,
+    fs,
     s1s,
     s1r,
     s2s,
@@ -99,17 +107,17 @@
     br,
     load,
     out,
+    chunk_out,
 ):
     d, m, y, x, c, px, py, pc = place()
     rows = x_ref.shape[0]
     half = rows // 2
-    shards = (wa_in, wu_in, wd_in)
-
-    def part(w, mk, ys, xs, core, start, size):
+
+    def part(w, s, ys, xs, core, start, size):
         if w == 0:
-            return wa.at[ys, xs, pl.ds(mk * 192 + core * 96 + start, size)]
+            return wa.at[ys, xs, pl.ds(s * 192 + core * 96 + start, size)]
         full = wu if w == 1 else wd
-        return full.at[mk, ys, xs, pl.ds(core * 96 + start, size)]
+        return full.at[s, ys, xs, pl.ds(core * 96 + start, size)]
 
     every = slice(None)
 
@@ -118,103 +126,175 @@
             src_ref=src, dst_ref=dst, send_sem=send, recv_sem=recv, device_id=peer, device_id_type=MESH
         )
 
-    def z_copy(w, k):
-        src = shards[w].at[y, x, pl.ds(c * 96, 96)]
-        return remote(src, part(w, m, y, x, c, 0, 96), zs.at[w, k - 1], zr.at[w, k - 1], (d, other_z(m, k)))
+    inner = (m == 1) | (m == 2)
+    k2 = 2 + ((m + 1) // 2) % 2
+    k3 = 5 - k2
+
+    def z_views(w, s):
+        if w < 2:
+            return (part(w, s, y, x, c, 0, 96),)
+        return part(w, s, every, x, c, 0, 48), part(w, s, y, every, c, 48, 48)
+
+    def z_copies(w, k):
+        peer = (d, other_z(m, k))
+        return [remote(v, v, zs.at[w, k - 1, h], zr.at[w, k - 1, h], peer) for h, v in enumerate(z_views(w, m))]
+
+    def z_forwards(w, k):
+        peer = (d, other_z(m, 1))
+        views = z_views(w, other_z(m, k))
+        return [remote(v, v, fs.at[w, k - 2, h], zr.at[w, 4 - k, h], peer) for h, v in enumerate(views)]
+
+    def z_begin(w):
+        for k in (1, k2):
+            for one in z_copies(w, k):
+                one.start()
 
     def z_wait(w, k):
-        here = part(w, other_z(m, k), y, x, c, 0, 96)
-        remote(here, here, zs.at[w, k - 1], zr.at[w, k - 1], (d, other_z(m, k))).wait_recv()
-
-    def s1(w, k, h):
-        mk = other_z(m, k)
-        here = part(w, mk, y, x, c, 48 * h, 48)
+        s = other_z(m, k)
+        for h, v in enumerate(z_views(w, s)):
+            remote(v, v, zs.at[w, k - 1, h], zr.at[w, k - 1, h], (d, s)).wait_recv()
+
+    def forward(w, k):
+        @pl.when(inner)
+        def _():
+            z_wait(w, k)
+            for one in z_forwards(w, k):
+                one.start()
+
+    def arrive(w, k):
+        if isinstance(k, int):
+            z_wait(w, k)
+        else:
+
+            @pl.when((m == 0) | (m == 3))
+            def _():
+                z_wait(w, k)
+
+    def s1(w, s, h):
+        here = part(w, s, y, x, c, 48 * h, 48)
         peer = (px, m) if h == 0 else (py, m)
-        return remote(here, here, s1s.at[w, k - 1, h], s1r.at[w, k - 1, h], peer)
-
-    def s1_wait(w, k, h):
-        mk = other_z(m, k)
-        here = part(w, mk, y, 1 - x, c, 0, 48) if h == 0 else part(w, mk, 1 - y, x, c, 48, 48)
+        return remote(here, here, s1s.at[w, s, h], s1r.at[w, s, h], peer)
+
+    def s1_wait(w, s, h):
+        here = part(w, s, y, 1 - x, c, 0, 48) if h == 0 else part(w, s, 1 - y, x, c, 48, 48)
         peer = (px, m) if h == 0 else (py, m)
-        remote(here, here, s1s.at[w, k - 1, h], s1r.at[w, k - 1, h], peer).wait_recv()
-
-    def s2(w, k, h):
-        mk = other_z(m, k)
-        here = part(w, mk, y, every, c, 0, 48) if h == 0 else part(w, mk, every, x, c, 48, 48)
+        remote(here, here, s1s.at[w, s, h], s1r.at[w, s, h], peer).wait_recv()
+
+    def s2(w, s, h):
+        here = part(w, s, y, every, c, 0, 48) if h == 0 else part(w, s, every, x, c, 48, 48)
         peer = (py, m) if h == 0 else (px, m)
-        return remote(here, here, s2s.at[w, k - 1, h], s2r.at[w, k - 1, h], peer)
-
-    def s2_wait(w, k, h):
-        mk = other_z(m, k)
-        here = part(w, mk, 1 - y, every, c, 0, 48) if h == 0 else part(w, mk, every, 1 - x, c, 48, 48)
+        return remote(here, here, s2s.at[w, s, h], s2r.at[w, s, h], peer)
+
+    def s2_wait(w, s, h):
+        here = part(w, s, 1 - y, every, c, 0, 48) if h == 0 else part(w, s, every, 1 - x, c, 48, 48)
         peer = (py, m) if h == 0 else (px, m)
-        remote(here, here, s2s.at[w, k - 1, h], s2r.at[w, k - 1, h], peer).wait_recv()
-
-    def core(w, k):
-        here = part(w, other_z(m, k), every, every, c, 0, 96)
-        return remote(here, here, cs.at[w, k - 1], cr.at[w, k - 1], (pc, m))
+        remote(here, here, s2s.at[w, s, h], s2r.at[w, s, h], peer).wait_recv()
+
+    def core(w, s):
+        here = part(w, s, every, every, c, 0, 96)
+        return remote(here, here, cs.at[w, s], cr.at[w, s], (pc, m))
 
     def core_wait(w, k):
-        here = part(w, other_z(m, k), every, every, 1 - c, 0, 96)
-        remote(here, here, cs.at[w, k - 1], cr.at[w, k - 1], (pc, m)).wait_recv()
+        s = other_z(m, k)
+        here = part(w, s, every, every, 1 - c, 0, 96)
+        remote(here, here, cs.at[w, s], cr.at[w, s], (pc, m)).wait_recv()
 
     def go1(w, k):
-        z_wait(w, k)
-        s1(w, k, 0).start()
-        s1(w, k, 1).start()
+        s = other_z(m, k)
+        arrive(w, k)
+        if w < 2:
+            s1(w, s, 0).start()
+            s1(w, s, 1).start()
+        else:
+            last(s, 0).start()
+            last(s, 1).start()
+
+    def last(s, h):
+        here = part(2, s, every, x, c, 0, 48) if h == 0 else part(2, s, y, every, c, 48, 48)
+        peer = (px, m) if h == 0 else (py, m)
+        return remote(here, here, s2s.at[2, s, h], s2r.at[2, s, h], peer)
+
+    def last_wait(s, h):
+        here = part(2, s, every, 1 - x, c, 0, 48) if h == 0 else part(2, s, 1 - y, every, c, 48, 48)
+        peer = (px, m) if h == 0 else (py, m)
+        remote(here, here, s2s.at[2, s, h], s2r.at[2, s, h], peer).wait_recv()
 
     def go2(w, k):
-        s1_wait(w, k, 0)
-        s1_wait(w, k, 1)
-        s2(w, k, 0).start()
-        s2(w, k, 1).start()
+        s = other_z(m, k)
+        s1_wait(w, s, 0)
+        s2(w, s, 0).start()
+        s1_wait(w, s, 1)
+        s2(w, s, 1).start()
 
     def go3(w, k):
-        s2_wait(w, k, 0)
-        s2_wait(w, k, 1)
-        core(w, k).start()
+        s = other_z(m, k)
+        wait = functools.partial(s2_wait, w) if w < 2 else last_wait
+        wait(s, 0)
+        wait(s, 1)
+        core(w, s).start()
 
     def own(w):
-        return pltpu.make_async_copy(shards[w], part(w, m, every, every, 0, 0, 192), load.at[w])
+        if w == 0:
+            mine = pl.ds(m * 192, 192)
+            return [pltpu.make_async_copy(wq_in.at[t], wa.at[t // 2, t % 2, mine], load.at[t]) for t in range(3)] + [
+                pltpu.make_async_copy(wo_in, wa.at[1, 1, mine], load.at[3])
+            ]
+        src = wu_in if w == 1 else wd_in
+        return [pltpu.make_async_copy(src, part(w, m, every, every, 0, 0, 192), load.at[3 + w])]
 
     def bias_copy(k):
-        return remote(bias_in, bias.at[m], bs.at[k - 1], br.at[k - 1], (d, other_z(m, k)))
+        return remote(bias.at[m], bias.at[m], bs.at[k - 1], br.at[k - 1], (d, other_z(m, k)))
 
     def bias_wait(k):
         here = bias.at[other_z(m, k)]
         remote(here, here, bs.at[k - 1], br.at[k - 1], (d, other_z(m, k))).wait_recv()
 
+    for w in range(3):
+        for one in own(w):
+            one.start()
+    bias[m, 0:1] = up_bias[...].reshape(1, 768)
+    bias[m, 1:3] = qv_bias[...]
+    bias[m, 3:8] = jnp.zeros((5, 768), F32)
     enter(d, m, px, py, pc)
-    for k in (1, 2, 3):
-        z_copy(0, k).start()
+    for one in own(0):
+        one.wait()
+    z_begin(0)
     for k in (1, 2, 3):
         bias_copy(k).start()
-    for w in range(3):
-        own(w).start()
-    own_bias = pltpu.make_async_copy(bias_in, bias.at[m], load.at[3])
-    own_bias.start()
+    for one in own(1):
+        one.wait()
+    z_begin(1)
 
     def norm(values, gain, shift):
         center = values - jnp.mean(values, axis=-1, keepdims=True)
         inverse = lax.rsqrt(jnp.mean(center * center, axis=-1, keepdims=True) + EPS)
         return center * inverse * gain + shift
 
-    n1_s[...] = norm(x_ref[...].astype(F32), vec_ref[0:1], vec_ref[1:2]).astype(BF)
+    def blocks(body):
+        for i in range(rows // 32):
+            body(pl.ds(i * 32, 32))
+
+    def first_norm(block):
+        n1_s[block] = norm(x_ref[block].astype(F32), gain1[...].reshape(1, 768), shift1[...].reshape(1, 768)).astype(BF)
+
+    blocks(first_norm)
     save = [pltpu.make_async_copy(n1_s, n1_out, out.at[0])]
     save[0].start()
+    for one in own(2):
+        one.wait()
 
     go1(0, 1)
+    forward(0, 3)
+    forward(0, 2)
+    z_begin(2)
+    go1(0, k2)
     go2(0, 1)
-    go1(0, 2)
-    go1(0, 3)
-    for k in (1, 2, 3):
-        z_copy(1, k).start()
+    forward(1, 3)
+    go1(0, k3)
+    go1(1, 1)
+    go2(0, k2)
+    forward(1, 2)
     go3(0, 1)
-    go2(0, 2)
-    go2(0, 3)
-    for w in range(3):
-        own(w).wait()
-    own_bias.wait()
     for k in (1, 2, 3):
         bias_wait(k)
     core_wait(0, 1)
@@ -222,7 +302,7 @@
     group0 = m // 2
     key_row = lax.broadcasted_iota(jnp.int32, (rows, LANES), 0)
     lane = lax.broadcasted_iota(jnp.int32, (rows, LANES), 1)
-    mask_add = jnp.where(key_row < fill_ref[0], 0.0, MASKED)
+    mask_add = jnp.where(key_row < fill_ref[m], 0.0, MASKED)
     lane_half = lax.broadcasted_iota(jnp.int32, (half, LANES), 1)
 
     def project(g):
@@ -270,54 +350,88 @@
             ho_s[block, lanes] = jnp.where(lane_half < HD, mixed[0], mixed[1]).astype(BF)
 
     project(group0)
-    go3(0, 2)
-    go3(0, 3)
+
+    def steps(j, lists):
+        for i, todo in enumerate(lists):
+
+            @pl.when(j == i)
+            def _(todo=todo):
+                for stage, w, k in todo:
+                    stage(w, k)
 
     def first_group(j, carry):
         attend(group0 * 3 + j)
-        go1(1, j + 1)
+        steps(
+            j,
+            (
+                ((go2, 0, k3), (go3, 0, k2), (go1, 1, k2), (go2, 1, 1), (forward, 2, 3)),
+                ((go3, 0, k3), (go1, 1, k3), (go2, 1, k2), (forward, 2, 2), (go1, 2, 1)),
+                ((go3, 1, 1), (go2, 1, k3)),
+            ),
+        )
         return carry
 
     lax.fori_loop(0, 3, first_group, 0)
-    for k in (1, 2, 3):
-        z_copy(2, k).start()
-    for k in (1, 2, 3):
-        go2(1, k)
     core_wait(0, 2)
     core_wait(0, 3)
+    save.append(pltpu.make_async_copy(wa, wa_out, out.at[7]))
+    save[-1].start()
     project(1 - group0)
 
     def second_group(j, carry):
         attend((1 - group0) * 3 + j)
-        go3(1, j + 1)
-        go1(2, j + 1)
+        steps(j, (((go3, 1, k2), (go1, 2, k2)), ((go3, 1, k3), (go3, 2, 1)), ((go1, 2, k3),)))
         return carry
 
     lax.fori_loop(0, 3, second_group, 0)
-    for k in (1, 2, 3):
-        go2(2, k)
     pairs = ((qa_s, qa_out), (k_s, k_out), (v_s, v_out), (ho_s, ho_out))
     for i, (a, b) in enumerate(pairs):
         save.append(pltpu.make_async_copy(a, b, out.at[1 + i]))
         save[-1].start()
-    r1 = x_ref[...].astype(F32) + dot(ho_s[...], wa[1, 1], NN) + vec_ref[2:3]
-    r1_s[...] = r1
-    n2_s[...] = norm(r1, vec_ref[3:4], vec_ref[4:5]).astype(BF)
-    acc[...] = r1 + vec_ref[5:6]
-    more = ((r1_s, r1_out), (n2_s, n2_out), (wa, wa_out))
+
+    def finish_attention(n, carry):
+        cols = pl.ds(pl.multiple_of(n * 256, 256), 256)
+        acc[:, cols] = dot(ho_s[...], wa[1, 1, :, cols], NN)
+        return carry
+
+    lax.fori_loop(0, 3, finish_attention, 0)
+
+    def second_norm(block):
+        r1 = x_ref[block].astype(F32) + acc[block] + out_bias[...].reshape(1, 768)
+        r1_s[block] = r1
+        n2_s[block] = norm(r1, gain2[...].reshape(1, 768), shift2[...].reshape(1, 768)).astype(BF)
+        acc[block] = r1 + down_bias[...].reshape(1, 768)
+
+    blocks(second_norm)
+    more = ((r1_s, r1_out), (n2_s, n2_out))
     for i, (a, b) in enumerate(more):
         save.append(pltpu.make_async_copy(a, b, out.at[5 + i]))
         save[-1].start()
-    for k in (1, 2, 3):
-        go3(2, k)
+    go3(2, k2)
+
+    def in_order(k):
+        return k + (k // 2) * (k2 - 2) * (5 - 2 * k)
+
+    def chunk_save(k):
+        mk = other_z(m, in_order(k))
+        pairs = ((wu, wu_out), (wd, wd_out), (hid_s, hid_out), (gp_s, gp_out))
+        return [pltpu.make_async_copy(a.at[mk], b.at[mk], chunk_out.at[i, k]) for i, (a, b) in enumerate(pairs)]
 
     def feed(k, carry):
-        mk = other_z(m, k)
+        ke = in_order(k)
+        mk = other_z(m, ke)
+
+        @pl.when(k == 1)
+        def _():
+            go3(2, k3)
 
         @pl.when(k > 0)
         def _():
-            core_wait(1, k)
-            core_wait(2, k)
+            core_wait(1, ke)
+            core_wait(2, ke)
+
+        for one in chunk_save(k)[:2]:
+            one.start()
 
         def up(n, inner):
             cols = pl.ds(pl.multiple_of(n * 256, 256), 256)
@@ -331,6 +445,8 @@
             return inner
 
         lax.fori_loop(0, 3, up, 0)
+        for one in chunk_save(k)[2:]:
+            one.start()
 
         def down(n, inner):
             cols = pl.ds(pl.multiple_of(n * 256, 256), 256)
@@ -343,24 +459,38 @@
 
     lax.fori_loop(0, 4, feed, 0)
     lo_s[...] = acc[...].astype(BF)
-    last = ((hid_s, hid_out), (gp_s, gp_out), (wu, wu_out), (wd, wd_out), (lo_s, layer_out))
-    for i, (a, b) in enumerate(last):
-        save.append(pltpu.make_async_copy(a, b, out.at[8 + i]))
-        save[-1].start()
+    save.append(pltpu.make_async_copy(lo_s, layer_out, out.at[8]))
+    save[-1].start()
     for one in save:
         one.wait()
+    for k in range(4):
+        for one in chunk_save(k):
+            one.wait()
     for k in (1, 2, 3):
         bias_copy(k).wait_send()
     for w in range(3):
         for k in (1, 2, 3):
-            z_copy(w, k).wait_send()
+            s = other_z(m, k)
             for h in (0, 1):
-                s1(w, k, h).wait_send()
-                s2(w, k, h).wait_send()
-            core(w, k).wait_send()
-
-
-def forward_call(fill, x, wa, wu, wd, bias, vec):
+                if w < 2:
+                    s1(w, s, h).wait_send()
+                    s2(w, s, h).wait_send()
+                else:
+                    last(s, h).wait_send()
+            core(w, s).wait_send()
+
+        for k in (1, k2):
+            for one in z_copies(w, k):
+                one.wait_send()
+
+        @pl.when(inner)
+        def _(w=w):
+            for k in (2, 3):
+                for one in z_forwards(w, k):
+                    one.wait_send()
+
+
+def forward_call(fill, x, weights, vectors):
     rows, width = x.shape
     any_spec = pl.BlockSpec(memory_space=pl.ANY)
     vmem = pl.BlockSpec(memory_space=pltpu.VMEM)
@@ -402,33 +532,36 @@
         pltpu.VMEM((4, rows, 768), BF),
         pltpu.VMEM((4, rows, 768), BF),
         pltpu.VMEM(flat, BF),
-        dma((3, 3)),
-        dma((3, 3)),
         dma((3, 3, 2)),
         dma((3, 3, 2)),
-        dma((3, 3, 2)),
-        dma((3, 3, 2)),
-        dma((3, 3)),
-        dma((3, 3)),
+        dma((3, 2, 2)),
+        dma((3, 4, 2)),
+        dma((3, 4, 2)),
+        dma((3, 4, 2)),
+        dma((3, 4, 2)),
+        dma((3, 4)),
+        dma((3, 4)),
         dma((3,)),
         dma((3,)),
-        dma((4,)),
-        dma((13,)),
+        dma((6,)),
+        dma((9,)),
+        dma((4, 4)),
     ]
     return pl.pallas_call(
         forward_kernel,
         out_shape=outs,
-        in_specs=[pl.BlockSpec(memory_space=pltpu.SMEM), vmem, any_spec, any_spec, any_spec, any_spec, vmem],
+        in_specs=[pl.BlockSpec(memory_space=pltpu.SMEM), vmem] + [any_spec] * 4 + [vmem] * 8,
         out_specs=[any_spec] * len(outs),
         scratch_shapes=scratch,
         compiler_params=pltpu.CompilerParams(collective_id=0, has_side_effects=True, vmem_limit_bytes=60 << 20),
         name="forward",
-    )(fill, x, wa, wu, wd, bias, vec)
+    )(fill, x, *weights, *vectors)
 
 
 def backward_kernel(
     fill_ref,
-    vec_ref,
+    gain1,
+    gain2,
     lo_in,
     g_in,
     x_in,
@@ -536,16 +669,33 @@
                     def _(up=up, j=j):
                         self.copy(up, 1, j, True).start()
 
-        def relay(self, dist, j):
-            for up in (True, False):
-                @pl.when(self.gets(up, dist))
+        def pass_on(self, up, dist, j):
+            self.copy(up, dist, j, False).wait_recv()
+            self.copy(up, dist + 1, j, True).start()
+
+        def outward(self, dist, j):
+            for at, up in ((1, False), (2, True)):
+                @pl.when(m == at)
                 def _(up=up):
-                    self.copy(up, dist, j, False).wait_recv()
-
-                if dist < 3:
-                    @pl.when(self.sends(up, dist + 1))
-                    def _(up=up):
-                        self.copy(up, dist + 1, j, True).start()
+                    self.pass_on(up, dist, j)
+
+        def inward(self, j):
+            for at, up in ((1, True), (2, False)):
+                @pl.when(m == at)
+                def _(up=up):
+                    self.pass_on(up, 1, j)
+
+        def rest(self):
+            for dist in (1, 2, 3):
+                for j in range(4):
+                    for up in (True, False):
+                        stays = self.gets(up, dist)
+                        if dist < 3:
+                            stays = stays & ((m == 3) if up else (m == 0))
+
+                        @pl.when(stays)
+                        def _(up=up, dist=dist, j=j):
+                            self.copy(up, dist, j, False).wait_recv()
 
         def finish(self):
             for dist in (1, 2, 3):
@@ -568,8 +718,33 @@
             return remote(unit.at[a, u, 1 - y, x, c, pl.ds(0, 48)], ry.at[a, u, 0], s2s.at[a, u, 0], s2r.at[a, u, 0], (py, m))
         return remote(unit.at[a, u, y, 1 - x, c, pl.ds(48, 48)], ry.at[a, u, 1], s2s.at[a, u, 1], s2r.at[a, u, 1], (px, m))
 
-    def z_send(a, u):
-        return remote(unit.at[a, u, y, x, c], rz.at[a, u - 1], zs.at[a, u - 1], zr.at[a, u - 1], (d, other_z(m, u)))
+    def z_send(a, up, dist):
+        p = m + dist if up else m - dist
+        slot = 4 if (up and dist == 1) else p
+        peer = m + 1 if up else m - 1
+        return remote(unit.at[a, other_z(m, p), y, x, c], rz.at[a, slot], zs.at[a, p], zr.at[a, slot], (d, peer))
+
+    def z_recv(a, slot):
+        remote(rz.at[a, slot], rz.at[a, slot], zs.at[a, 0], zr.at[a, slot], (d, other_z(m, 1))).wait_recv()
+
+    def z_has(up, dist):
+        return (m + dist <= 3) if up else (m >= dist)
+
+    def z_step(a, dist):
+        for up in (True, False):
+
+            @pl.when(z_has(up, dist))
+            def _(up=up):
+                p = m + dist if up else m - dist
+                if dist < 3:
+
+                    @pl.when((m > 0) if up else (m < 3))
+                    def _():
+                        z_recv(a, p)
+                        u = other_z(m, p)
+                        unit[a, u, y, x, c] = (unit[a, u, y, x, c].astype(F32) + rz[a, p].astype(F32)).astype(BF)
+
+                z_send(a, up, dist).start()
 
     def go1(a, u):
         core_send(a, u).wait_recv()
@@ -591,16 +766,18 @@
             part = pl.ds(48 * h, 48)
             unit[a, u, y, x, c, part] = (unit[a, u, y, x, c, part].astype(F32) + ry[a, u, h].astype(F32)).astype(BF)
 
-        @pl.when(u > 0)
+    def go4(a):
+        grads[a] = unit[a, 0, y, x, c].astype(F32)
+
+        @pl.when(m < 3)
         def _():
-            z_send(a, u).start()
-
-    def go4(a):
-        total = unit[a, 0, y, x, c].astype(F32)
-        for k in (1, 2, 3):
-            z_send(a, k).wait_recv()
-            total = total + rz[a, k - 1].astype(F32)
-        grads[a] = total
+            z_recv(a, m)
+            grads[a] += rz[a, m].astype(F32)
+
+        @pl.when(m > 0)
+        def _():
+            z_recv(a, 4)
+            grads[a] += rz[a, 4].astype(F32)
 
     def copies(i):
         pairs = (
@@ -680,14 +857,19 @@
             acc[:, cols] += dot(pre_s[...], wu_b[slot, cols], NT)
             return inner
 
+        @pl.when(k > 0)
+        def _():
+            go1(0, u + 1)
+            go1(1, u + 1)
+
         lax.fori_loop(0, 3, third, 0)
-        go1(0, u)
-        go1(1, u)
         return carry
 
     lax.fori_loop(0, 4, feed, 0)
-    for j in range(4):
-        line_lo.relay(1, j)
+    line_lo.outward(1, 0)
+    line_lo.inward(0)
+    line_lo.outward(1, 1)
+    line_lo.inward(1)
 
     def norm_back(values, upstream, gain):
         center = values - jnp.mean(values, axis=-1, keepdims=True)
@@ -703,19 +885,23 @@
     for i in (2, 3, 4):
         copies(i).wait()
 
-    def second_norm(i, carry):
-        block = pl.ds(pl.multiple_of(i * 32, 32), 32)
+    zero = jnp.zeros((1, 768), F32)
+    carry = (zero, zero, zero, zero)
+    for i in range(rows // 32):
+        block = pl.ds(i * 32, 32)
         upstream = acc[block]
-        through, gain_part, shift_part = norm_back(r1_s[block], upstream, vec_ref[3:4])
+        through, gain_part, shift_part = norm_back(r1_s[block], upstream, gain2[...].reshape(1, 768))
         g = g_s[block].astype(F32)
         res = g + through
         r1_s[block] = res
         res_s[block] = res.astype(BF)
         parts = (gain_part, shift_part, jnp.sum(res, axis=0, keepdims=True), jnp.sum(g, axis=0, keepdims=True))
-        return tuple(a + b for a, b in zip(carry, parts))
-
-    zero = jnp.zeros((1, 768), F32)
-    n2g, n2s, ob, db = lax.fori_loop(0, rows // 32, second_norm, (zero, zero, zero, zero))
+        carry = tuple(a + b for a, b in zip(carry, parts))
+    n2g, n2s, ob, db = carry
+    go1(0, 0)
+    go1(1, 0)
+    line_lo.outward(1, 2)
+    line_lo.inward(2)
     vs0[2:3] = ob
     vs0[3:4] = n2g
     vs0[4:5] = n2s
@@ -727,12 +913,14 @@
         return carry
 
     lax.fori_loop(0, 3, heads_grad, 0)
+    line_lo.outward(1, 3)
+    line_lo.inward(3)
     for i in (5, 6, 7):
         copies(i).wait()
 
     key_row = lax.broadcasted_iota(jnp.int32, (rows, LANES), 0)
     lane = lax.broadcasted_iota(jnp.int32, (rows, LANES), 1)
-    mask_add = jnp.where(key_row < fill_ref[0], 0.0, MASKED)
+    mask_add = jnp.where(key_row < fill_ref[m], 0.0, MASKED)
     lane_half = lax.broadcasted_iota(jnp.int32, (half, LANES), 1)
     lane_turned = lax.broadcasted_iota(jnp.int32, (LANES, rows), 0)
 
@@ -779,24 +967,31 @@
     def pair(p, carry):
         attend(p)
 
-        @pl.when(p < 4)
+        @pl.when((p == 1) | (p == 3))
         def _():
-            go2(0, 3 - p)
-            go2(1, 3 - p)
-
-        @pl.when(p >= 2)
+            u = 3 - p // 2
+            go2(0, u)
+            go2(1, u)
+
+        @pl.when(p == 5)
         def _():
-            go3(0, 5 - p)
-            go3(1, 5 - p)
+            go3(0, 3)
+            go3(1, 3)
 
         for j in range(4):
             @pl.when(p == j + 1)
             def _(j=j):
-                line_lo.relay(2, j)
+                line_lo.outward(2, j)
 
         return carry
 
     lax.fori_loop(0, 6, pair, 0)
+    def both(stage, u):
+        stage(0, u)
+        stage(1, u)
+
+    both(go2, 1)
+    both(z_step, 3)
     vs0[6:7] = jnp.sum(dq_s[...].astype(F32), axis=0, keepdims=True)
     vs0[7:8] = jnp.sum(dv_s[...].astype(F32), axis=0, keepdims=True)
     copies(8).wait()
@@ -810,16 +1005,18 @@
         return carry
 
     lax.fori_loop(0, 3, last_product, 0)
-
-    def first_norm(i, carry):
-        block = pl.ds(pl.multiple_of(i * 32, 32), 32)
-        through, gain_part, shift_part = norm_back(x_s[block].astype(F32), acc[block], vec_ref[0:1])
+    both(go3, 2)
+
+    carry = (zero, zero)
+    for i in range(rows // 32):
+        block = pl.ds(i * 32, 32)
+        through, gain_part, shift_part = norm_back(x_s[block].astype(F32), acc[block], gain1[...].reshape(1, 768))
         dho_s[block] = (r1_s[block] + through).astype(BF)
-        return tuple(a + b for a, b in zip(carry, (gain_part, shift_part)))
-
-    n1g, n1s = lax.fori_loop(0, rows // 32, first_norm, (zero, zero))
+        carry = (carry[0] + gain_part, carry[1] + shift_part)
+    n1g, n1s = carry
     vs0[0:1] = n1g
     vs0[1:2] = n1s
+    both(z_step, 2)
     line_pg.begin()
     own_pg = pltpu.make_async_copy(dho_s, pg_all.at[m], own_sem.at[1])
     own_pg.start()
@@ -860,50 +1057,68 @@
         core_send(2, other_z(m, 2 * e + 1)).start()
         return carry
 
-    lax.fori_loop(0, 2, attention_grads, 0)
-
-    def run(stage, start=3):
-        def body(i, carry):
-            stage(2, 3 - i)
-            return carry
-
-        lax.fori_loop(0, 4, body, 0)
-
-    run(go1)
+    attention_grads(0, 0)
+    both(go2, 0)
+    both(go3, 1)
+    attention_grads(1, 0)
 
     peers = ((pc, m), (px, m), (py, m))
 
     def small(i):
         return remote(vs0, vs_r.at[i], vss.at[i], vsr.at[i], peers[i])
 
-    for i in range(3):
-        small(i).start()
+    def small_add(i):
         small(i).wait()
         vs0[...] += vs_r[i]
 
     def small_z(k):
         return remote(vs0, vs_z.at[k - 1], vzs.at[k - 1], vzr.at[k - 1], (d, other_z(m, k)))
 
+    small(0).start()
+    for u in (3, 2, 1, 0):
+        go1(2, u)
+    line_pg.outward(1, 0)
+    both(z_step, 1)
+    small_add(0)
+    small(1).start()
+    line_pg.outward(1, 1)
+    both(go3, 0)
+    small_add(1)
+    small(2).start()
+    go2(2, 3)
+    line_pg.outward(1, 2)
+    go2(2, 2)
+    small_add(2)
     for k in (1, 2, 3):
         small_z(k).start()
-    run(go2)
-    run(go3)
-    for j in range(4):
-        line_pg.relay(1, j)
-    for j in range(4):
-        line_lo.relay(3, j)
-    for j in range(4):
-        line_pg.relay(2, j)
-    go4(0)
-    go4(1)
-    go4(2)
+    line_pg.inward(0)
+    line_pg.outward(1, 3)
+    go2(2, 1)
+    go3(2, 3)
+    z_step(2, 3)
+    line_pg.inward(1)
+    go2(2, 0)
+    go3(2, 2)
+    line_pg.inward(2)
+    line_pg.outward(2, 0)
+    go3(2, 1)
+    line_pg.inward(3)
+    line_pg.outward(2, 1)
+    go3(2, 0)
+    z_step(2, 2)
+    line_pg.outward(2, 2)
+    line_pg.outward(2, 3)
+    z_step(2, 1)
+    line_lo.rest()
     total = vs0[...]
     for k in (1, 2, 3):
         small_z(k).wait_recv()
         total = total + vs_z[k - 1]
     sums[...] = total
-    for j in range(4):
-        line_pg.relay(3, j)
+    go4(0)
+    go4(1)
+    go4(2)
+    line_pg.rest()
     line_lo.finish()
     line_pg.finish()
     own_lo.wait()
@@ -916,11 +1131,15 @@
             for h in (0, 1):
                 s1(a, u, h).wait_send()
                 s2(a, u, h).wait_send()
-            if u > 0:
-                z_send(a, u).wait_send()
-
-
-def backward_call(fill, vec, lo, g, x, qa, k, v, ho, n1, n2, r1, hid, gp, wa, wu, wd):
+        for dist in (1, 2, 3):
+            for up in (True, False):
+
+                @pl.when(z_has(up, dist))
+                def _(a=a, dist=dist, up=up):
+                    z_send(a, up, dist).wait_send()
+
+
+def backward_call(fill, gain1, gain2, lo, g, x, qa, k, v, ho, n1, n2, r1, hid, gp, wa, wu, wd):
     rows, width = x.shape
     any_spec = pl.BlockSpec(memory_space=pl.ANY)
     vmem = pl.BlockSpec(memory_space=pltpu.VMEM)
@@ -958,7 +1177,7 @@
         pltpu.VMEM((3, 4, 2, 2, 96, 768), BF),
         pltpu.VMEM((3, 4, 2, 2, 48, 768), BF),
         pltpu.VMEM((3, 4, 2, 48, 768), BF),
-        pltpu.VMEM((3, 3, 96, 768), BF),
+        pltpu.VMEM((3, 5, 96, 768), BF),
         pltpu.VMEM((16, width), F32),
         pltpu.VMEM((3, 16, width), F32),
         pltpu.VMEM((3, 16, width), F32),
@@ -972,8 +1191,8 @@
         dma((3, 4, 2)),
         dma((3, 4, 2)),
         dma((3, 4, 2)),
-        dma((3, 3)),
-        dma((3, 3)),
+        dma((3, 4)),
+        dma((3, 5)),
         dma((3,)),
         dma((3,)),
         dma((3,)),
@@ -985,12 +1204,12 @@
     return pl.pallas_call(
         backward_kernel,
         out_shape=outs,
-        in_specs=[pl.BlockSpec(memory_space=pltpu.SMEM), vmem] + [any_spec] * 15,
+        in_specs=[pl.BlockSpec(memory_space=pltpu.SMEM), vmem, vmem] + [any_spec] * 15,
         out_specs=[any_spec, any_spec, vmem, vmem],
         scratch_shapes=scratch,
         compiler_params=pltpu.CompilerParams(collective_id=1, has_side_effects=True, vmem_limit_bytes=62 << 20),
         name="backward",
-    )(fill, vec, lo, g, x, qa, k, v, ho, n1, n2, r1, hid, gp, wa, wu, wd)
+    )(fill, gain1, gain2, lo, g, x, qa, k, v, ho, n1, n2, r1, hid, gp, wa, wu, wd)
 
 
 def prepare(patches, fill_lengths, cotangent, norm1_gain, norm1_shift, w_qkv, qv_bias, w_out, out_bias, norm2_gain, norm2_shift, w_up, up_bias, w_down, down_bias):
@@ -1000,25 +1219,26 @@
     pad = ((0, rows - length), (0, 0))
     x = jnp.pad(lax.dynamic_index_in_dim(patches, m, 0, keepdims=False), pad)
     cot = jnp.pad(lax.dynamic_index_in_dim(cotangent, m, 0, keepdims=False), pad)
-    fill = lax.dynamic_slice(fill_lengths, (m,), (1,))
-    wa = jnp.concatenate([jnp.transpose(w_qkv, (1, 2, 0)).reshape(576, width), w_out], axis=0)
-    wa = wa.reshape(2, 2, 192, width)
-    wu = w_up.reshape(2, 2, 192, width)
-    wd = w_down.reshape(2, 2, 192, width)
-    placed = lax.dynamic_update_slice(jnp.zeros((2, width), F32), qv_bias, (0, m * 192))
-    bias = jnp.concatenate([up_bias[None], placed, jnp.zeros((5, width), F32)], axis=0)
-    zero = jnp.zeros_like(norm1_gain)
-    vec = jnp.stack([norm1_gain, norm1_shift, out_bias, norm2_gain, norm2_shift, down_bias, zero, zero])
-    return x, cot, fill, wa, wu, wd, bias, vec
+    weights = (
+        jnp.transpose(w_qkv, (1, 2, 0)),
+        w_out,
+        w_up.reshape(2, 2, 192, width),
+        w_down.reshape(2, 2, 192, width),
+    )
+    owner = lax.broadcasted_iota(jnp.int32, (2, 768), 1) // 192
+    placed = jnp.where(owner == m, jnp.tile(qv_bias, (1, 4)), 0.0)
+    vectors = (placed, up_bias, norm1_gain, norm1_shift, out_bias, norm2_gain, norm2_shift, down_bias)
+    return x, cot, weights, vectors
 
 
 def one_item(*args):
     length, width = args[0].shape[1:]
-    x, cot, fill, wa, wu, wd, bias, vec = prepare(*args)
-    lo, qa, k, v, ho, n1, n2, r1, hid, gp, wa, wu, wd = forward_call(fill, x, wa, wu, wd, bias, vec)
+    x, cot, weights, vectors = prepare(*args)
+    fill = args[1]
+    lo, qa, k, v, ho, n1, n2, r1, hid, gp, wa, wu, wd = forward_call(fill, x, weights, vectors)
     wu = wu.reshape(4, width, 768)
     wd = wd.reshape(4, 768, width)
-    lo_all, pg_all, grads, sums = backward_call(fill, vec, lo, cot, x, qa, k, v, ho, n1, n2, r1, hid, gp, wa, wu, wd)
+    lo_all, pg_all, grads, sums = backward_call(fill, vectors[2], vectors[5], lo, cot, x, qa, k, v, ho, n1, n2, r1, hid, gp, wa, wu, wd)
     d = lax.axis_index("dp")
     m = lax.axis_index("mp")
     layer_out = lo_all[:, :length]

time: 276 us -> 232 us (0.84)
  Pallas kernels: 238 us -> 203 us
  local copies, waits for them, and re-layouts: 32.2 us -> 23.7 us
    pallas_call x1, Pallas kernels: 156 us -> 133 us  [backward_call(): pl.pallas_call(backward_kernel, out_shape=outs, in_specs=[pl.BlockSpec(me...]
    pallas_call x1, Pallas kernels: 82.1 us -> 70.4 us  [forward_call(): pl.pallas_call(forward_kernel, out_shape=outs, in_specs=[pl.BlockSpec(mem...]
    another operation x9 -> x2, local copies, waits for them, and re-layouts: 4.79 us -> 0.09 us  [prepare(): placed = jnp.where(owner == m, jnp.tile(qv_bias, (1, 4)), 0.0)]
    concatenate x2 -> x0, other arithmetic: 3.03 us -> none  [the longest x1 2.35 us: prepare(): jnp.concatenate([jnp.transpose(w_qkv, (1, 2, 0)).reshape(576, width), w_o...]
where the time goes in v3:
time: 232 us
  Pallas kernels  203 us (88%)
  local copies, waits for them, and re-layouts  23.7 us (10%)
  other arithmetic  4.08 us (2%)
    pallas_call x1, Pallas kernels, backward_call(): pl.pallas_call(backward_kernel, out_shape=outs, in_specs=[pl.BlockSpec(me...  133 us
    pallas_call x1, Pallas kernels, forward_call(): pl.pallas_call(forward_kernel, out_shape=outs, in_specs=[pl.BlockSpec(mem...  70.4 us
    unnamed x9, local copies, waits for them, and re-layouts  9.22 us
    dynamic_slice x1, local copies, waits for them, and re-layouts, prepare(): lax.dynamic_index_in_dim(cotangent, m, 0, keepdims=False)  6.26 us

profile of v3, /device:TPU:0, one launch (start us, length us, event | category | flops | bytes accessed | tf_op | source)
XLA Modules:
  0.0 231.9 jit_solution(5164762724895927126)
XLA Ops:
  0.6 6.3 %constant_dynamic-slice_fusion.1 = (bf16[1,529,768]{2,0,1:T(2,128)(2,1)S(1)}, bf16[1,529,768]{2,0,1:T(2,128)(2,1)S(1)}) fusion(bf16[4,529,768]{2,0,1:T(4,128)(2,1)} %param.17, s32[]{:T(128)S(6)} %select_n.60, bf16[4,529,768]{2,0,1:T(4,128)(2,1)} %param.15), kind=kLoop, calls=%fused_computation.26 | loop fusion | bytes 3250180 | tf_op jit(solution)/shard_map/jit(dynamic_index_in_dim)/dynamic_slice | solution.py:1221
  6.9 0.1 copy.42
  7.0 1.0 pad.7.x_ref.x_in
  8.0 0.1 tile.10
  8.1 0.6 compare_select_fusion.qv_bias
  8.7 70.4 %forward.1 = (bf16[544,768]{1,0:T(8,128)(2,1)}, bf16[12,544,128]{2,1,0:T(8,128)(2,1)}, bf16[544,768]{1,0:T(8,128)(2,1)}, bf16[544,768]{1,0:T(8,128)(2,1)}, bf16[...) custom-call(s32[4]{0:T(128)} %fill_ref.3, ...), custom_call_target="tpu_custom_call" | custom-call | tf_op jit(solution)/shard_map/forward/pallas_call | solution.py:550
  79.1 0.1 copy.41
  79.2 1.0 pad.8.g_in
  80.2 132.9 %backward.1 = (bf16[4,544,768]{2,1,0:T(8,128)(2,1)}, bf16[4,544,768]{2,1,0:T(8,128)(2,1)}, f32[3,96,768]{2,1,0:T(8,128)}, f32[16,768]{1,0:T(8,128)}) custom-call(s32[4]{0:T(128)} %fill_ref.3, f32[768]{0:T(1024)} %gain1.3, f32[768]{0:T(1024)} %gain2.3, bf16[544,768]{1,0:T(8,128)(2,1)} %get-tuple-element.31.lo_in, bf16[544,768]{1,0:T(8,128)(2,1)} %pad.8.g_in, ...), custom_call_target="tpu_custom_call" | custom-call | tf_op jit(solution)/shard_map/backward/pallas_call | solution.py:1204
  213.1 2.0 slice_bitcast_fusion
  215.2 0.1 fusion.6
  215.3 0.1 fusion.2
  215.4 0.7 copy.36
  216.1 0.1 maximum_select_fusion
  216.2 0.1 fusion.1
  216.4 0.7 pad_maximum_fusion
  217.1 2.4 %slice_convert_fusion = f32[4,529,768]{2,1,0:T(8,128)S(1)} fusion(bf16[4,544,768]{2,1,0:T(8,128)(2,1)} %get-tuple-element.45), kind=kLoop, calls=%fused_computation | loop fusion | flops 1625088 | bytes 9750528 | tf_op jit(solution)/shard_map/convert_element_type | solution.py:1245
  219.5 5.3 %copy.35 = f32[4,529,768]{2,0,1:T(4,128)} copy(f32[4,529,768]{2,1,0:T(8,128)S(1)} %slice_convert_fusion) | data formatting | bytes 13000704
  224.8 0.2 slice.71
  225.0 3.0 %copy.34 = bf16[4,529,768]{2,0,1:T(4,128)(2,1)} copy(bf16[4,529,768]{2,1,0:T(8,128)(2,1)S(1)} %slice.71) | data formatting | bytes 6500352
  228.0 1.3 constant_dynamic-slice_fusion.3
  229.3 1.3 dynamic-slice_bitcast_fusion
  230.6 0.8 constant_dynamic-slice_fusion
  231.4 0.5 slice_bitcast_fusion.6
  (8 shorter events, 0.0 us)
Async XLA Ops:
  6.9 1.1 copy-start.1
  219.5 5.3 %copy-start = (bf16[4,544,768]{2,1,0:T(8,128)(2,1)S(1)}, bf16[4,544,768]{2,1,0:T(8,128)(2,1)}, u32[]{:S(2)}) copy-start(bf16[4,544,768]{2,1,0:T(8,128)(2,1)} %get-tuple-element.44) | copy-start | bytes 10027012

commit v4 on v3

--- a/solution.py
+++ b/solution.py
@@ -52,7 +52,8 @@
 
 def forward_kernel(
     fill_ref,
-    x_ref,
+    x_in,
+    g_in,
     wq_in,
     wo_in,
     wu_in,
@@ -78,6 +79,8 @@
     wa_out,
     wu_out,
     wd_out,
+    x_out,
+    g_out,
     wa,
     wu,
     wd,
@@ -94,6 +97,10 @@
     hid_s,
     gp_s,
     lo_s,
+    x_s,
+    g_s,
+    raw_x,
+    raw_g,
     zs,
     zr,
     fs,
@@ -110,7 +117,8 @@
     chunk_out,
 ):
     d, m, y, x, c, px, py, pc = place()
-    rows = x_ref.shape[0]
+    rows = x_s.shape[0]
+    length = x_in.shape[0]
     half = rows // 2
 
     def part(w, s, ys, xs, core, start, size):
@@ -252,6 +260,12 @@
     for w in range(3):
         for one in own(w):
             one.start()
+    items = [
+        pltpu.make_async_copy(src, dst.at[pl.ds(0, length)], load.at[6 + i])
+        for i, (src, dst) in enumerate(((x_in, raw_x), (g_in, raw_g)))
+    ]
+    for one in items:
+        one.start()
     bias[m, 0:1] = up_bias[...].reshape(1, 768)
     bias[m, 1:3] = qv_bias[...]
     bias[m, 3:8] = jnp.zeros((5, 768), F32)
@@ -274,12 +288,36 @@
         for i in range(rows // 32):
             body(pl.ds(i * 32, 32))
 
+    def take(raw, item, i):
+        block = pl.ds(pl.multiple_of(i * 32, 32), 32)
+        v = raw[block].astype(F32)
+        which = lax.broadcasted_iota(jnp.int32, v.shape, 1)
+        row = lax.broadcasted_iota(jnp.int32, v.shape, 0) + i * 32
+        item[block] = jnp.sum(jnp.where((which == m) & (row < length), v, 0.0), axis=1).astype(BF)
+
+    items[0].wait()
+
+    def take_x(i, carry):
+        take(raw_x, x_s, i)
+        return carry
+
+    lax.fori_loop(0, rows // 32, take_x, 0)
+
     def first_norm(block):
-        n1_s[block] = norm(x_ref[block].astype(F32), gain1[...].reshape(1, 768), shift1[...].reshape(1, 768)).astype(BF)
+        n1_s[block] = norm(x_s[block].astype(F32), gain1[...].reshape(1, 768), shift1[...].reshape(1, 768)).astype(BF)
 
     blocks(first_norm)
     save = [pltpu.make_async_copy(n1_s, n1_out, out.at[0])]
     save[0].start()
+    items[1].wait()
+
+    def take_g(p):
+        for i in range(3):
+
+            @pl.when(3 * p + i < rows // 32)
+            def _(i=i):
+                take(raw_g, g_s, 3 * p + i)
+
     for one in own(2):
         one.wait()
 
@@ -361,6 +399,7 @@
 
     def first_group(j, carry):
         attend(group0 * 3 + j)
+        take_g(j)
         steps(
             j,
             (
@@ -380,6 +419,7 @@
 
     def second_group(j, carry):
         attend((1 - group0) * 3 + j)
+        take_g(3 + j)
         steps(j, (((go3, 1, k2), (go1, 2, k2)), ((go3, 1, k3), (go3, 2, 1)), ((go1, 2, k3),)))
         return carry
 
@@ -388,6 +428,9 @@
     for i, (a, b) in enumerate(pairs):
         save.append(pltpu.make_async_copy(a, b, out.at[1 + i]))
         save[-1].start()
+    for i, (a, b) in enumerate(((x_s, x_out), (g_s, g_out))):
+        save.append(pltpu.make_async_copy(a, b, out.at[9 + i]))
+        save[-1].start()
 
     def finish_attention(n, carry):
         cols = pl.ds(pl.multiple_of(n * 256, 256), 256)
@@ -397,7 +440,7 @@
     lax.fori_loop(0, 3, finish_attention, 0)
 
     def second_norm(block):
-        r1 = x_ref[block].astype(F32) + acc[block] + out_bias[...].reshape(1, 768)
+        r1 = x_s[block].astype(F32) + acc[block] + out_bias[...].reshape(1, 768)
         r1_s[block] = r1
         n2_s[block] = norm(r1, gain2[...].reshape(1, 768), shift2[...].reshape(1, 768)).astype(BF)
         acc[block] = r1 + down_bias[...].reshape(1, 768)
@@ -490,8 +533,9 @@
                     one.wait_send()
 
 
-def forward_call(fill, x, weights, vectors):
-    rows, width = x.shape
+def forward_call(fill, x, g, weights, vectors):
+    length, items, width = x.shape
+    rows = -(-length // 32) * 32
     any_spec = pl.BlockSpec(memory_space=pl.ANY)
     vmem = pl.BlockSpec(memory_space=pltpu.VMEM)
     flat = (rows, width)
@@ -513,6 +557,8 @@
         hbm((2, 2, 768, 768)),
         hbm((4, 2, 2, 192, 768)),
         hbm((4, 2, 2, 192, 768)),
+        hbm(flat),
+        hbm(flat),
     ]
     dma = pltpu.SemaphoreType.DMA
     scratch = [
@@ -532,6 +578,10 @@
         pltpu.VMEM((4, rows, 768), BF),
         pltpu.VMEM((4, rows, 768), BF),
         pltpu.VMEM(flat, BF),
+        pltpu.VMEM(flat, BF),
+        pltpu.VMEM(flat, BF),
+        pltpu.VMEM((rows, items, width), BF),
+        pltpu.VMEM((rows, items, width), BF),
         dma((3, 3, 2)),
         dma((3, 3, 2)),
         dma((3, 2, 2)),
@@ -543,19 +593,19 @@
         dma((3, 4)),
         dma((3,)),
         dma((3,)),
-        dma((6,)),
-        dma((9,)),
+        dma((8,)),
+        dma((11,)),
         dma((4, 4)),
     ]
     return pl.pallas_call(
         forward_kernel,
         out_shape=outs,
-        in_specs=[pl.BlockSpec(memory_space=pltpu.SMEM), vmem] + [any_spec] * 4 + [vmem] * 8,
+        in_specs=[pl.BlockSpec(memory_space=pltpu.SMEM)] + [any_spec] * 6 + [vmem] * 8,
         out_specs=[any_spec] * len(outs),
         scratch_shapes=scratch,
         compiler_params=pltpu.CompilerParams(collective_id=0, has_side_effects=True, vmem_limit_bytes=60 << 20),
         name="forward",
-    )(fill, x, *weights, *vectors)
+    )(fill, x, g, *weights, *vectors)
 
 
 def backward_kernel(
@@ -1214,11 +1264,9 @@
 
 def prepare(patches, fill_lengths, cotangent, norm1_gain, norm1_shift, w_qkv, qv_bias, w_out, out_bias, norm2_gain, norm2_shift, w_up, up_bias, w_down, down_bias):
     m = lax.axis_index("mp")
-    length, width = patches.shape[1:]
-    rows = -(-length // 32) * 32
-    pad = ((0, rows - length), (0, 0))
-    x = jnp.pad(lax.dynamic_index_in_dim(patches, m, 0, keepdims=False), pad)
-    cot = jnp.pad(lax.dynamic_index_in_dim(cotangent, m, 0, keepdims=False), pad)
+    width = patches.shape[2]
+    x = jnp.transpose(patches, (1, 0, 2))
+    cot = jnp.transpose(cotangent, (1, 0, 2))
     weights = (
         jnp.transpose(w_qkv, (1, 2, 0)),
         w_out,
@@ -1235,7 +1283,7 @@
     length, width = args[0].shape[1:]
     x, cot, weights, vectors = prepare(*args)
     fill = args[1]
-    lo, qa, k, v, ho, n1, n2, r1, hid, gp, wa, wu, wd = forward_call(fill, x, weights, vectors)
+    lo, qa, k, v, ho, n1, n2, r1, hid, gp, wa, wu, wd, x, cot = forward_call(fill, x, cot, weights, vectors)
     wu = wu.reshape(4, width, 768)
     wd = wd.reshape(4, 768, width)
     lo_all, pg_all, grads, sums = backward_call(fill, vectors[2], vectors[5], lo, cot, x, qa, k, v, ho, n1, n2, r1, hid, gp, wa, wu, wd)

time: 232 us -> 224 us (0.966)
  local copies, waits for them, and re-layouts: 23.7 us -> 16 us
    dynamic_slice x1 -> x0, local copies, waits for them, and re-layouts: 6.26 us -> none  [prepare(): lax.dynamic_index_in_dim(cotangent, m, 0, keepdims=False)]
    pallas_call x1, Pallas kernels: 133 us -> 131 us  [backward_call(): pl.pallas_call(backward_kernel, out_shape=outs, in_specs=[pl.BlockSpec(me...]
    unnamed x9 -> x5, local copies, waits for them, and re-layouts: 9.22 us -> 8.98 us
where the time goes in v4:
time: 224 us; the launch traced here: 222 us
  Pallas kernels  202 us (90%)
  local copies, waits for them, and re-layouts  16 us (7%)
  other arithmetic  4.08 us (2%)
    pallas_call x1, Pallas kernels, backward_call(): pl.pallas_call(backward_kernel, out_shape=outs, in_specs=[pl.BlockSpec(me...  131 us
    pallas_call x1, Pallas kernels, forward_call(): pl.pallas_call(forward_kernel, out_shape=outs, in_specs=[pl.BlockSpec(mem...  71.1 us
    unnamed x5, local copies, waits for them, and re-layouts  8.98 us

profile of v4, /device:TPU:0, one launch (start us, length us, event | category | flops | bytes accessed | tf_op | source)
XLA Modules:
  0.0 222.5 jit_solution(13399446352809345466)
XLA Ops:
  0.7 0.7 tile.4
  1.3 0.1 tile.10
  1.4 0.6 compare_select_fusion.qv_bias
  2.1 71.1 %forward.1 = (bf16[544,768]{1,0:T(8,128)(2,1)}, bf16[12,544,128]{2,1,0:T(8,128)(2,1)}, bf16[544,768]{1,0:T(8,128)(2,1)}, bf16[544,768]{1,0:T(8,128)(2,1)}, bf16[...) custom-call(s32[4]{0:T(128)} %fill_ref.3, ...), custom_call_target="tpu_custom_call" | custom-call | tf_op jit(solution)/shard_map/forward/pallas_call | solution.py:600
  73.2 130.5 %backward.1 = (bf16[4,544,768]{2,1,0:T(8,128)(2,1)}, bf16[4,544,768]{2,1,0:T(8,128)(2,1)}, f32[3,96,768]{2,1,0:T(8,128)}, f32[16,768]{1,0:T(8,128)}) custom-call(s32[4]{0:T(128)} %fill_ref.3, f32[768]{0:T(1024)} %gain1.3, f32[768]{0:T(1024)} %gain2.3, bf16[544,768]{1,0:T(8,128)(2,1)} %get-tuple-element.33.lo_in, bf16[544,768]{1,0:T(8,128)(2,1)} %get-tuple-element.34.g_in, ...), custom_call_target="tpu_custom_call" | custom-call | tf_op jit(solution)/shard_map/backward/pallas_call | solution.py:1254
  203.7 2.0 slice_bitcast_fusion
  205.7 0.1 fusion.6
  205.9 0.1 fusion.2
  206.0 0.7 copy.31
  206.7 0.1 maximum_select_fusion
  206.8 0.1 fusion.1
  206.9 0.7 pad_maximum_fusion
  207.7 2.4 %slice_convert_fusion = f32[4,529,768]{2,1,0:T(8,128)S(1)} fusion(bf16[4,544,768]{2,1,0:T(8,128)(2,1)} %get-tuple-element.49), kind=kLoop, calls=%fused_computation | loop fusion | flops 1625088 | bytes 9750528 | tf_op jit(solution)/shard_map/convert_element_type | solution.py:1293
  210.1 0.0 copy-start
  210.1 5.3 %copy.30 = f32[4,529,768]{2,0,1:T(4,128)} copy(f32[4,529,768]{2,1,0:T(8,128)S(1)} %slice_convert_fusion) | data formatting | bytes 13000704
  215.4 0.0 copy-done
  215.4 0.2 slice.71
  215.6 3.0 %copy.29 = bf16[4,529,768]{2,0,1:T(4,128)(2,1)} copy(bf16[4,529,768]{2,1,0:T(8,128)(2,1)S(1)} %slice.71) | data formatting | bytes 6500352
  218.6 1.3 constant_dynamic-slice_fusion
  219.9 1.3 dynamic-slice_bitcast_fusion
  221.2 0.8 constant_dynamic-slice_fusion.1
  222.0 0.5 slice_bitcast_fusion.6
  (3 shorter events, 0.0 us)
Async XLA Ops:
  210.1 5.3 %copy-start = (bf16[4,544,768]{2,1,0:T(8,128)(2,1)S(1)}, bf16[4,544,768]{2,1,0:T(8,128)(2,1)}, u32[]{:S(2)}) copy-start(bf16[4,544,768]{2,1,0:T(8,128)(2,1)} %get-tuple-element.48) | copy-start | bytes 10027012

commit v5 on v4

--- a/solution.py
+++ b/solution.py
@@ -267,8 +267,13 @@
     for one in items:
         one.start()
     bias[m, 0:1] = up_bias[...].reshape(1, 768)
-    bias[m, 1:3] = qv_bias[...]
-    bias[m, 3:8] = jnp.zeros((5, 768), F32)
+    bias[m, 1:8] = jnp.zeros((7, 768), F32)
+    for plane in range(4):
+
+        @pl.when(m == plane)
+        def _(plane=plane):
+            bias[plane, 1:3, plane * 192 : (plane + 1) * 192] = qv_bias[...]
+
     enter(d, m, px, py, pc)
     for one in own(0):
         one.wait()
@@ -1164,7 +1169,21 @@
     for k in (1, 2, 3):
         small_z(k).wait_recv()
         total = total + vs_z[k - 1]
-    sums[...] = total
+    up = jnp.zeros((1, 768), F32)
+    for plane in range(4):
+        up = jnp.where(m == plane, total[8 + plane : 9 + plane], up)
+    rows_of = jnp.concatenate([total[0:8], up, jnp.zeros((7, 768), F32)], axis=0)
+    mine = jnp.zeros((16, 96), F32)
+    for i in range(8):
+        mine = jnp.where(d == i, rows_of[:, i * 96 : (i + 1) * 96], mine)
+    sums[0:16, 0:96] = mine
+    of_plane = jnp.zeros((8, 192), F32)
+    for plane in range(4):
+        of_plane = jnp.where(m == plane, total[0:8, plane * 192 : (plane + 1) * 192], of_plane)
+    few = jnp.zeros((8, 24), F32)
+    for i in range(8):
+        few = jnp.where(d == i, of_plane[:, i * 24 : (i + 1) * 24], few)
+    sums[16:24, 0:24] = few
     go4(0)
     go4(1)
     go4(2)
@@ -1198,7 +1217,7 @@
         jax.ShapeDtypeStruct((4, rows, width), BF),
         jax.ShapeDtypeStruct((4, rows, width), BF),
         jax.ShapeDtypeStruct((3, 96, 768), F32),
-        jax.ShapeDtypeStruct((16, width), F32),
+        jax.ShapeDtypeStruct((24, LANES), F32),
     ]
     dma = pltpu.SemaphoreType.DMA
     scratch = [
@@ -1273,9 +1292,7 @@
         w_up.reshape(2, 2, 192, width),
         w_down.reshape(2, 2, 192, width),
     )
-    owner = lax.broadcasted_iota(jnp.int32, (2, 768), 1) // 192
-    placed = jnp.where(owner == m, jnp.tile(qv_bias, (1, 4)), 0.0)
-    vectors = (placed, up_bias, norm1_gain, norm1_shift, out_bias, norm2_gain, norm2_shift, down_bias)
+    vectors = (qv_bias, up_bias, norm1_gain, norm1_shift, out_bias, norm2_gain, norm2_shift, down_bias)
     return x, cot, weights, vectors
 
 
@@ -1287,7 +1304,6 @@
     wu = wu.reshape(4, width, 768)
     wd = wd.reshape(4, 768, width)
     lo_all, pg_all, grads, sums = backward_call(fill, vectors[2], vectors[5], lo, cot, x, qa, k, v, ho, n1, n2, r1, hid, gp, wa, wu, wd)
-    d = lax.axis_index("dp")
     m = lax.axis_index("mp")
     layer_out = lo_all[:, :length]
     patches_grad = pg_all[:, :length].astype(F32)
@@ -1304,9 +1320,9 @@
     k_grad = pick([(256, 384), (192, 256)], [(64, 128), (256, 384)])
     v_grad = pick([(384, 576)], [(384, 448), (512, 640)])
     o_grad = pick([(640, 768), (576, 640)], [(448, 512), (640, 768)])
-    mine = lax.dynamic_slice(sums, (0, d * 96), (8, 96))
-    qv = lax.dynamic_slice(sums, (6, m * 192 + d * 24), (2, 24))
-    up_grad = lax.dynamic_slice(sums, (8 + m, d * 96), (1, 96))[0]
+    mine = sums[0:9, 0:96]
+    qv = sums[22:24, 0:24]
+    up_grad = mine[8]
     return (
         layer_out,
         patches_grad,

time: 224 us -> 222 us (level)
  no operation moved by 1% of the time
where the time goes in v5:
time: 222 us; the launch traced here: 220 us
  Pallas kernels  202 us (91%)
  local copies, waits for them, and re-layouts  14 us (6%)
  other arithmetic  3.45 us (2%)
    pallas_call x1, Pallas kernels, backward_call(): pl.pallas_call(backward_kernel, out_shape=outs, in_specs=[pl.BlockSpec(me...  131 us
    pallas_call x1, Pallas kernels, forward_call(): pl.pallas_call(forward_kernel, out_shape=outs, in_specs=[pl.BlockSpec(mem...  71.3 us
    unnamed x5, local copies, waits for them, and re-layouts  8.98 us

profile of v5, /device:TPU:0, one launch (start us, length us, event | category | flops | bytes accessed | tf_op | source)
XLA Modules:
  0.0 220.1 jit_solution(9851872669242136742)
XLA Ops:
  0.6 71.3 %forward.1 = (bf16[544,768]{1,0:T(8,128)(2,1)}, bf16[12,544,128]{2,1,0:T(8,128)(2,1)}, bf16[544,768]{1,0:T(8,128)(2,1)}, bf16[544,768]{1,0:T(8,128)(2,1)}, bf16[...) custom-call(s32[4]{0:T(128)} %fill_ref.3, ...), custom_call_target="tpu_custom_call" | custom-call | tf_op jit(solution)/shard_map/forward/pallas_call | solution.py:605
  72.0 130.6 %backward.1 = (bf16[4,544,768]{2,1,0:T(8,128)(2,1)}, bf16[4,544,768]{2,1,0:T(8,128)(2,1)}, f32[3,96,768]{2,1,0:T(8,128)}, f32[24,128]{1,0:T(8,128)}) custom-call(s32[4]{0:T(128)} %fill_ref.3, f32[768]{0:T(1024)} %gain1.3, f32[768]{0:T(1024)} %gain2.3, bf16[544,768]{1,0:T(8,128)(2,1)} %get-tuple-element.33.lo_in, bf16[544,768]{1,0:T(8,128)(2,1)} %get-tuple-element.34.g_in, ...), custom_call_target="tpu_custom_call" | custom-call | tf_op jit(solution)/shard_map/backward/pallas_call | solution.py:1273
  202.5 2.0 slice_bitcast_fusion
  204.6 0.1 fusion.3
  204.7 0.1 fusion.2
  204.8 0.7 copy.31
  205.5 0.1 maximum_select_fusion
  205.6 0.1 fusion.1
  205.8 0.7 pad_maximum_fusion
  206.5 2.4 %slice_convert_fusion = f32[4,529,768]{2,1,0:T(8,128)S(1)} fusion(bf16[4,544,768]{2,1,0:T(8,128)(2,1)} %get-tuple-element.49), kind=kLoop, calls=%fused_computation | loop fusion | flops 1625088 | bytes 9750528 | tf_op jit(solution)/shard_map/convert_element_type | solution.py:1309
  208.9 0.0 copy-start
  208.9 5.3 %copy.30 = f32[4,529,768]{2,0,1:T(4,128)} copy(f32[4,529,768]{2,1,0:T(8,128)S(1)} %slice_convert_fusion) | data formatting | bytes 13000704
  214.2 0.0 copy-done
  214.2 0.2 slice.85
  214.4 3.0 %copy.29 = bf16[4,529,768]{2,0,1:T(4,128)(2,1)} copy(bf16[4,529,768]{2,1,0:T(8,128)(2,1)S(1)} %slice.85) | data formatting | bytes 6500352
  217.4 1.4 slice_bitcast_fusion.6
  218.8 1.2 slice.99
  (1 shorter events, 0.0 us)
Async XLA Ops:
  208.9 5.3 %copy-start = (bf16[4,544,768]{2,1,0:T(8,128)(2,1)S(1)}, bf16[4,544,768]{2,1,0:T(8,128)(2,1)}, u32[]{:S(2)}) copy-start(bf16[4,544,768]{2,1,0:T(8,128)(2,1)} %get-tuple-element.48) | copy-start | bytes 10027012
